TPU v7x, 32 devices: a whole 2x2x4 slice. The times are simulated.
32 devices in a mesh: seq: 16 (over z, y, core), head: 2 (over x).
Axes of the slice: x: 2, y: 2, z: 4, core: 2. Of those that a mesh axis runs over, the one named last changes fastest.
Arguments:
- mixer_query: bfloat16 [4096, 4096], P('seq', 'head'), may hold values from -13 to 13
- mixer_key: bfloat16 [4096, 4096], P('seq', 'head'), may hold values from -6 to 6
- mixer_value: bfloat16 [4096, 4096], P('seq', 'head'), may hold values from -6 to 6
- shift_taps: float32 [8, 4096], P(None, 'head'), may hold values from -2 to 2
- conv_kernel: float32 [4096, 4096], P(('head', 'seq')), may hold values from -2 to 2
- heads_query: bfloat16 [4096, 4096], P('seq', 'head'), may hold values from -6 to 6
- heads_key: bfloat16 [4096, 4096], P('seq', 'head'), may hold values from -6 to 6
- heads_value: bfloat16 [4096, 4096], P('seq', 'head'), may hold values from -6 to 6
- beta_attention: float32 [4096], P('head'), may hold values from 0.5 to 2
- beta_mixer: float32 [4096], P('head'), may hold values from 0.5 to 2
Outputs:
- block_output: bfloat16 [4096, 4096], P('seq', 'head')
All inputs are finite; a program needn't handle non-finite values.
Results may differ from a plain program's by a relative error of at most 0.0053.
Values may be sent and summed in bfloat16 or wider, within the bound.
A program may use at most 128 MiB of HBM per device.

v0:
```python
import math

import jax
import jax.numpy as jnp
from jax import lax
from jax.sharding import PartitionSpec as P

D = 4096
HD = 128
TAPS = 8
SPAN = 3


exact_mode = lax.Precision.HIGHEST


def shifted_2(block, axis, distance):
    devices = range(lax.axis_size(axis))
    route = [(i - distance, i) for i in devices if i - distance in devices]
    return lax.ppermute(block, axis, route)


def shift_sum(extended, taps, count, axis):
    width = taps.shape[0]
    source = extended.astype(jnp.float32)
    total = jnp.zeros_like(lax.slice_in_dim(source, 0, count, axis=axis))
    for offset in range(width):
        window = lax.slice_in_dim(source, width - 1 - offset, width - 1 - offset + count, axis=axis)
        total = total + jnp.expand_dims(taps[offset], axis) * window
    return total


def angle_table(first_count, second_count, period):
    left = jnp.arange(first_count, dtype=jnp.int32)[:, None]
    right = jnp.arange(second_count, dtype=jnp.int32)[None, :]
    phase = (left * right % period).astype(jnp.float32) * (2.0 * math.pi / period)
    return (jnp.cos(phase), jnp.sin(phase))


def long_conv(signal, kernel):
    number, length = signal.shape
    radix = 128
    upper = length // radix
    outer = 2 * upper
    period = outer * radix
    cos_one, sin_one = angle_table(upper, outer, outer)
    cos_twist, sin_twist = angle_table(outer, radix, period)
    cos_two, sin_two = angle_table(radix, radix, radix)
    stacked = jnp.concatenate([signal, kernel], 0).reshape(2 * number, upper, radix)
    real_a = jnp.einsum("cab,ak->ckb", stacked, cos_one, precision=exact_mode)
    imag_a = -jnp.einsum("cab,ak->ckb", stacked, sin_one, precision=exact_mode)
    real_b = real_a * cos_twist + imag_a * sin_twist
    imag_b = imag_a * cos_twist - real_a * sin_twist
    real_c = jnp.einsum("ckb,bm->ckm", real_b, cos_two, precision=exact_mode) + jnp.einsum(
        "ckb,bm->ckm", imag_b, sin_two, precision=exact_mode
    )
    imag_c = jnp.einsum("ckb,bm->ckm", imag_b, cos_two, precision=exact_mode) - jnp.einsum(
        "ckb,bm->ckm", real_b, sin_two, precision=exact_mode
    )
    real_sig, real_ker = (real_c[:number], real_c[number:])
    imag_sig, imag_ker = (imag_c[:number], imag_c[number:])
    real_prod = real_sig * real_ker - imag_sig * imag_ker
    imag_prod = real_sig * imag_ker + imag_sig * real_ker
    real_z = jnp.einsum("ckm,mb->ckb", real_prod, cos_two, precision=exact_mode) - jnp.einsum(
        "ckm,mb->ckb", imag_prod, sin_two, precision=exact_mode
    )
    imag_z = jnp.einsum("ckm,mb->ckb", imag_prod, cos_two, precision=exact_mode) + jnp.einsum(
        "ckm,mb->ckb", real_prod, sin_two, precision=exact_mode
    )
    real_w = real_z * cos_twist - imag_z * sin_twist
    imag_w = imag_z * cos_twist + real_z * sin_twist
    result = jnp.einsum("ckb,ak->cab", real_w, cos_one, precision=exact_mode) - jnp.einsum(
        "ckb,ak->cab", imag_w, sin_one, precision=exact_mode
    )
    return (result / period).reshape(number, length)


def attend(query, keys, values, first):
    count, width = query.shape
    heads = width // HD
    scale = 1.0 / math.sqrt(HD)
    seen = keys.shape[0]
    query_heads = query.reshape(count, heads, HD)
    key_heads = keys.reshape(seen, heads, HD)
    value_heads = values.reshape(seen, heads, HD)
    scores = (
        jnp.einsum("qhd,khd->hqk", query_heads, key_heads, preferred_element_type=jnp.float32)
        * scale
    )
    query_pos = first + jnp.arange(count, dtype=jnp.int32)
    key_pos = first - (seen - count) + jnp.arange(seen, dtype=jnp.int32)
    visible = (key_pos[None, :] <= query_pos[:, None]) & (key_pos[None, :] >= 0)
    scores = jnp.where(visible[None], scores, -1e30)
    top = jnp.max(scores, axis=2, keepdims=True)
    probs = jnp.exp(scores - top)
    weights = probs.astype(jnp.bfloat16)
    numer = jnp.einsum("hqk,khd->qhd", weights, value_heads, preferred_element_type=jnp.float32)
    total = jnp.sum(probs, axis=2)
    return (numer / jnp.transpose(total)[:, :, None]).reshape(count, width)


def on_device(
    mixer_query,
    mixer_key,
    mixer_value,
    shift_taps,
    conv_kernel,
    heads_query,
    heads_key,
    heads_value,
    beta_attention,
    beta_mixer,
):
    count, width = mixer_key.shape
    edge = mixer_key[count - (TAPS - 1) :]
    before = shifted_2(edge, "seq", 1)
    extended = jnp.concatenate([before, mixer_key], 0)
    shifted = shift_sum(extended, shift_taps, count, 0)
    ssm_input = (shifted * mixer_value.astype(jnp.float32)).astype(jnp.bfloat16)
    signal = lax.all_to_all(
        jnp.transpose(ssm_input), "seq", split_axis=0, concat_axis=1, tiled=True
    )
    filtered = long_conv(signal.astype(jnp.float32), conv_kernel).astype(jnp.bfloat16)
    returned = lax.all_to_all(filtered, "seq", split_axis=1, concat_axis=0, tiled=True)
    mixer_branch = mixer_query.astype(jnp.float32) * jnp.transpose(returned).astype(jnp.float32)
    earlier = []
    carried = (heads_key, heads_value)
    for step in range(SPAN):
        carried = shifted_2((carried[0], carried[1]), "seq", 1)
        earlier.insert(0, carried)
    keys = jnp.concatenate([pair[0] for pair in earlier] + [heads_key], 0)
    values = jnp.concatenate([pair[1] for pair in earlier] + [heads_value], 0)
    first = lax.axis_index("seq") * count
    attention_branch = attend(heads_query, keys, values, first)
    attention_sums, mixer_sums = lax.psum(
        (
            jnp.sum(attention_branch * attention_branch, axis=1),
            jnp.sum(mixer_branch * mixer_branch, axis=1),
        ),
        "head",
    )
    attention_scale = lax.rsqrt(attention_sums / D + 1e-05)
    mixer_scale = lax.rsqrt(mixer_sums / D + 1e-05)
    joined = (
        beta_attention[None, :] * attention_branch * attention_scale[:, None]
        + beta_mixer[None, :] * mixer_branch * mixer_scale[:, None]
    )
    return (joined * 0.5).astype(jnp.bfloat16)


def solution(mesh):
    return jax.shard_map(
        on_device,
        mesh=mesh,
        in_specs=(
            P("seq", "head"),
            P("seq", "head"),
            P("seq", "head"),
            P(None, "head"),
            P(("head", "seq"), None),
            P("seq", "head"),
            P("seq", "head"),
            P("seq", "head"),
            P("head"),
            P("head"),
        ),
        out_specs=P("seq", "head"),
        check_vma=False,
    )
```

profile of v0, /device:TPU:16, one launch (start us, length us, event | category | flops | bytes accessed | tf_op | source)
XLA Modules:
  0.0 279.2 jit_solution(12235671070868579060)
XLA Ops:
  4.1 2.9 %collective-permute-done.6 = bf16[7,2048]{1,0:T(8,128)(2,1)S(1)} collective-permute-done((bf16[7,2048]{1,0:T(8,128)(2,1)S(1)}, bf16[7,2048]{1,0:T(8,128)(2,1)S(1)}, u32[]{:S(2)}, u32[]{:S(2)}) %collective-permute-start.6) | collective-permute-done | bytes 28704 | tf_op jit(solution)/shard_map/ppermute | solution.py:20
  8.5 3.2 %fusion.46 = bf16[2048,256]{0,1:T(8,128)(2,1)S(1)} fusion(bf16[256,2048]{1,0:T(8,128)(2,1)} %param.12, f32[263,2048]{1,0:T(8,128)S(1)} %maximum_convert_fusion, f32[2048]{0:T(1024)S(1)} %bitcast.110, f32[2048]{0:T(1024)S(1)} %bitcast.111, f32[2048]{0:T(1024)S(1)} %bitcast.105, f32[2048]{0:T(1024)S(1)} %bitcast.106, f32[2048]{0:T(1024)S(1)} %bitcast.107, ...), kind=kLoop, calls=%fused_computation.64 | loop fusion | flops 9437184 | bytes 18939904 | tf_op jit(solution)/shard_map/transpose | solution.py:121
  13.1 5.3 %all-to-all-start = ((bf16[16,128,256]{2,1,0:T(8,128)(2,1)}), bf16[16,128,256]{2,1,0:T(8,128)(2,1)}, u32[]{:S(2)}, u32[]{:S(2)}) async-start(bf16[16,128,256]{2,1,0:T(8,128)(2,1)} %bitcast.16), calls=%async_computation | async-start | bytes 2097152 | tf_op jit(solution)/shard_map/all_to_all | solution.py:120
  21.8 3.3 %collective-permute-start = (bf16[256,2048]{1,0:T(8,128)(2,1)}, bf16[256,2048]{1,0:T(8,128)(2,1)}, u32[]{:S(2)}, u32[]{:S(2)}) collective-permute-start(bf16[256,2048]{1,0:T(8,128)(2,1)} %param.17), channel_id=1, source_target_pairs={{0,2},{2,4},{4,6},{6,8},{8,10},{10,12},{12,14},{14,16},{16,18},{18... | collective-permute-start | bytes 3145736 | tf_op jit(solution)/shard_map/ppermute | solution.py:20
  27.6 27.4 %collective-permute-done.3 = bf16[256,2048]{0,1:T(8,128)(2,1)} collective-permute-done((bf16[256,2048]{0,1:T(8,128)(2,1)}, bf16[256,2048]{0,1:T(8,128)(2,1)}, u32[]{:S(2)}, u32[]{:S(2)}) %collective-permute-start.3) | collective-permute-done | bytes 1048608 | tf_op jit(solution)/shard_map/ppermute | solution.py:20
  56.9 9.3 %collective-permute-done = bf16[256,2048]{1,0:T(8,128)(2,1)} collective-permute-done((bf16[256,2048]{1,0:T(8,128)(2,1)}, bf16[256,2048]{1,0:T(8,128)(2,1)}, u32[]{:S(2)}, u32[]{:S(2)}) %collective-permute-start) | collective-permute-done | bytes 1048608 | tf_op jit(solution)/shard_map/ppermute | solution.py:20
  74.3 5.4 %copy.75 = f32[256,32,128]{2,1,0:T(8,128)} copy(f32[256,32,128]{0,2,1:T(8,128)} %bitcast.98) | data formatting | bytes 8388608 | tf_op jit(solution)/shard_map/reshape | solution.py:49
  79.7 10.9 %fusion.83 = f32[64,256,128]{2,0,1:T(8,128)} fusion(f32[256,32,128]{2,1,0:T(8,128)} %copy.75), kind=kOutput, calls=%fused_computation.102 | convolution fusion | flops 805335040 | bytes 12582912 | tf_op jit(solution)/shard_map/cab,ak->ckb/dot_general | solution.py:51
  90.6 11.0 %add_bitcast_fusion = (f32[256,64,128]{2,1,0:T(8,128)S(1)}, f32[256,64,128]{2,1,0:T(8,128)S(1)}) fusion(f32[64,256,128]{2,0,1:T(8,128)} %fusion.83, f32[64,128]{1,0:T(8,128)S(1)} %get-tuple-element.25, f32[64,128]{1,0:T(8,128)S(1)} %get-tuple-element.26, f32[256,32,128]{2,1,0:T(8,128)S(1)} %copy-done.1), kind=kOutput, calls=%fused_computation.7 | convolution fusion | flops 820015104 | bytes 29425664 | tf_op jit(solution)/shard_map/cab,ak->ckb/dot_general | solution.py:50
  101.6 15.7 %fusion.11 = f32[256,64,128]{2,0,1:T(8,128)} fusion(f32[256,64,128]{2,1,0:T(8,128)S(1)} %get-tuple-element.8), kind=kOutput, calls=%fused_computation.14 | convolution fusion | flops 3221454848 | bytes 16777216 | tf_op jit(solution)/shard_map/ckb,bm->ckm/dot_general | solution.py:54
  117.3 14.1 %fusion.9 = f32[256,64,128]{2,0,1:T(8,128)S(1)} fusion(f32[256,64,128]{2,1,0:T(8,128)S(1)} %get-tuple-element.8), kind=kOutput, calls=%fused_computation.12 | convolution fusion | flops 3221454848 | bytes 16777216 | tf_op jit(solution)/shard_map/ckb,bm->ckm/dot_general | solution.py:57
  131.4 16.2 %fusion.21 = f32[256,64,128]{2,0,1:T(8,128)S(1)} fusion(f32[256,64,128]{2,0,1:T(8,128)} %fusion.11, f32[256,64,128]{2,1,0:T(8,128)S(1)} %get-tuple-element.7), kind=kOutput, calls=%fused_computation.31 | convolution fusion | flops 3223552000 | bytes 25165824 | tf_op jit(solution)/shard_map/ckb,bm->ckm/dot_general | solution.py:54
  147.7 15.8 %fusion.24 = f32[256,64,128]{2,0,1:T(8,128)} fusion(f32[256,64,128]{2,0,1:T(8,128)S(1)} %fusion.9, f32[256,64,128]{2,1,0:T(8,128)S(1)} %get-tuple-element.7), kind=kOutput, calls=%fused_computation.32 | convolution fusion | flops 3223552000 | bytes 25165824 | tf_op jit(solution)/shard_map/ckb,bm->ckm/dot_general | solution.py:57
  163.5 4.6 %multiply_add_fusion.1 = (f32[128,64,128]{2,0,1:T(8,128)S(1)}, f32[128,64,128]{2,0,1:T(8,128)S(1)}) fusion(f32[256,64,128]{2,0,1:T(8,128)} %fusion.24, f32[256,64,128]{2,0,1:T(8,128)S(1)} %fusion.21), kind=kLoop, calls=%fused_computation.29 | loop fusion | flops 6291456 | bytes 25165824 | tf_op jit(solution)/shard_map/add | solution.py:63
  168.1 3.8 %fusion.56 = f32[128,64,128]{2,0,1:T(8,128)S(1)} fusion(f32[128,64,128]{2,0,1:T(8,128)S(1)} %get-tuple-element.10), kind=kOutput, calls=%fused_computation.77 | convolution fusion | flops 1610842112 | bytes 8388608 | tf_op jit(solution)/shard_map/ckm,mb->ckb/dot_general | solution.py:64
  171.9 3.8 %fusion.54 = f32[128,64,128]{2,0,1:T(8,128)S(1)} fusion(f32[128,64,128]{2,0,1:T(8,128)S(1)} %get-tuple-element.9), kind=kOutput, calls=%fused_computation.75 | convolution fusion | flops 1610842112 | bytes 8388608 | tf_op jit(solution)/shard_map/ckm,mb->ckb/dot_general | solution.py:67
  175.7 3.8 %convolution_subtract_fusion = f32[128,64,128]{2,0,1:T(8,128)S(1)} fusion(f32[128,64,128]{2,0,1:T(8,128)S(1)} %fusion.56, f32[128,64,128]{2,0,1:T(8,128)S(1)} %get-tuple-element.9), kind=kOutput, calls=%fused_computation.34 | convolution fusion | flops 1611890688 | bytes 12582912 | tf_op jit(solution)/shard_map/ckm,mb->ckb/dot_general | solution.py:64
  179.6 2.4 collective-permute-start.5
  182.0 4.6 %multiply_subtract_fusion = (f32[128,64,128]{2,0,1:T(8,128)S(1)}, f32[128,64,128]{2,0,1:T(8,128)S(1)}) fusion(f32[128,64,128]{2,0,1:T(8,128)S(1)} %convolution_subtract_fusion, f32[64,128]{1,0:T(8,128)S(1)} %get-tuple-element.25, f32[64,128]{1,0:T(8,128)S(1)} %get-tuple-element.26, f32[128,64,128]{2,0,1:T(8,128)S(1)} %fusion.54, ...), kind=kOutput, calls=%fused_computation.28 | convolution fusion | flops 1618182144 | bytes 21037056 | tf_op jit(solution)/shard_map/ckm,mb->ckb/dot_general | solution.py:67
  186.6 4.6 %fusion.17 = f32[32,128,128]{2,0,1:T(8,128)S(1)} fusion(f32[128,64,128]{2,0,1:T(8,128)S(1)} %get-tuple-element.12), kind=kOutput, calls=%fused_computation.23 | convolution fusion | flops 402681856 | bytes 6291456 | tf_op jit(solution)/shard_map/ckb,ak->cab/dot_general | solution.py:72
  191.2 4.9 %fusion.40 = bf16[128,32,128]{2,1,0:T(8,128)(2,1)S(1)} fusion(f32[32,128,128]{2,0,1:T(8,128)S(1)} %fusion.17, f32[128,64,128]{2,0,1:T(8,128)S(1)} %get-tuple-element.11), kind=kOutput, calls=%fused_computation.58 | convolution fusion | flops 404254720 | bytes 7340032 | tf_op jit(solution)/shard_map/ckb,ak->cab/dot_general | solution.py:72
  197.9 5.8 %all-to-all-start.1 = ((bf16[128,16,256]{2,0,1:T(8,128)(2,1)}), bf16[128,16,256]{2,0,1:T(8,128)(2,1)S(1)}, u32[]{:S(2)}, u32[]{:S(2)}) async-start(bf16[128,16,256]{2,0,1:T(8,128)(2,1)} %copy.71), calls=%async_computation.1 | async-start | bytes 2097152 | tf_op jit(solution)/shard_map/all_to_all | solution.py:124
  205.8 2.5 pad_maximum_fusion.1
  208.3 7.5 %fusion.2 = (f32[16,256]{1,0:T(8,128)S(1)}, f32[16,1024,256]{2,1,0:T(8,128)}) fusion(pred[256,1024]{0,1:T(8,128)(4,1)S(1)} %compare_and_fusion, bf16[1024,16,128]{0,2,1:T(8,128)(2,1)S(1)} %bitcast.99, bf16[256,2048]{1,0:T(8,128)(2,1)S(1)} %copy-done), kind=kOutput, calls=%fused_computation.4 | convolution fusion | flops 1086320640 | bytes 22298624 | tf_op jit(solution)/shard_map/qhd,khd->hqk/dot_general | solution.py:87
  215.7 9.1 %fusion = f32[16,256]{1,0:T(8,128)S(1)} fusion(f32[16,1024,256]{2,1,0:T(8,128)} %get-tuple-element.22, f32[16,256]{1,0:T(8,128)S(1)} %get-tuple-element.21, pred[256,1024]{0,1:T(8,128)(4,1)S(1)} %compare_and_fusion), kind=kLoop, calls=%fused_computation.2 | loop fusion | flops 16773120 | bytes 17072128 | tf_op jit(solution)/shard_map/reduce_sum | solution.py:98
  224.8 15.4 %collective-permute-done.2 = bf16[256,2048]{1,0:T(8,128)(2,1)S(1)} collective-permute-done((bf16[256,2048]{1,0:T(8,128)(2,1)}, bf16[256,2048]{1,0:T(8,128)(2,1)S(1)}, u32[]{:S(2)}, u32[]{:S(2)}) %collective-permute-start.2) | collective-permute-done | bytes 1048608 | tf_op jit(solution)/shard_map/ppermute | solution.py:20
  240.2 3.5 %pad_maximum_fusion = bf16[1024,2048]{1,0:T(8,128)(2,1)} fusion(bf16[256,2048]{1,0:T(8,128)(2,1)} %param.17, bf16[256,2048]{1,0:T(8,128)(2,1)} %collective-permute-done, bf16[256,2048]{1,0:T(8,128)(2,1)} %collective-permute-done.1, bf16[256,2048]{1,0:T(8,128)(2,1)S(1)} %collective-permute-done.2), kind=kLoop, calls=%fused_computation.20 | loop fusion | flops 16777216 | bytes 8388608 | tf_op jit(solution)/shard_map/concatenate | solution.py:132
  243.7 6.4 %copy.54 = bf16[1024,2048]{0,1:T(8,128)(2,1)} copy(bf16[1024,2048]{1,0:T(8,128)(2,1)} %pad_maximum_fusion) | data formatting | bytes 8388608 | tf_op jit(solution)/shard_map/concatenate | solution.py:132
  250.2 12.4 %multiply_reduce_fusion.1 = (f32[256]{0:T(256)S(1)}, f32[256,16,128]{0,2,1:T(8,128)}) fusion(f32[256,16]{0,1:T(8,128)S(1)} %bitcast.112, bf16[1024,16,128]{0,2,1:T(8,128)(2,1)} %bitcast.102, f32[16,1024,256]{2,1,0:T(8,128)} %get-tuple-element.22, f32[16,256]{1,0:T(8,128)S(1)} %get-tuple-element.21, pred[256,1024]{0,1:T(8,128)(4,1)S(1)} %compare_and_fusion), kind=kOutput, calls=%fused_computation.57 | convolution fusion | flops 1092091648 | bytes 23364608 | tf_op jit(solution)/shard_map/hqk,khd->qhd/dot_general | solution.py:97
  262.6 2.9 %copy.60 = f32[256,2048]{1,0:T(8,128)} copy(f32[256,2048]{0,1:T(8,128)} %bitcast.103) | data formatting | bytes 4194304 | tf_op jit(solution)/shard_map/reshape | solution.py:99
  270.6 4.9 %all-reduce = (f32[256]{0:T(256)S(1)}, f32[256]{0:T(256)S(1)}) all-reduce(f32[256]{0:T(256)S(1)} %multiply_reduce_fusion, f32[256]{0:T(256)S(1)} %get-tuple-element.23), channel_id=1, replica_groups=mesh['seq'=16,'head'=2] {'head'}, use_global_device_ids=true, to_apply=%region_5.6 | all-reduce | flops 512 | bytes 4096 | tf_op jit(solution)/shard_map/psum | solution.py:135
  275.6 3.5 %multiply_convert_fusion = bf16[256,2048]{1,0:T(8,128)(2,1)} fusion(f32[256,2048]{1,0:T(8,128)} %copy.60, f32[2048,256]{0,1:T(8,128)S(1)} %copy.72, bf16[256,2048]{1,0:T(8,128)(2,1)} %param.10, f32[256]{0:T(256)S(1)} %add_rsqrt_fusion, f32[2048]{0:T(1024)S(1)} %copy-done.3, f32[256]{0:T(256)S(1)} %add_rsqrt_fusion.1, f32[2048]{0:T(1024)S(1)} %copy-done.4), kind=kLoop, calls=%fused_computation.54 | loop fusion | flops 4718592 | bytes 6309888 | tf_op jit(solution)/shard_map/convert_element_type | solution.py:148
  (41 shorter events, 31.6 us)
Async XLA Ops:
  0.0 208.3 %copy-start = (bf16[256,2048]{1,0:T(8,128)(2,1)S(1)}, bf16[256,2048]{1,0:T(8,128)(2,1)}, u32[]{:S(2)}) copy-start(bf16[256,2048]{1,0:T(8,128)(2,1)} %param.15) | copy-start | bytes 3145732
  0.9 6.1 %collective-permute-start.6 = (bf16[7,2048]{1,0:T(8,128)(2,1)S(1)}, bf16[7,2048]{1,0:T(8,128)(2,1)S(1)}, u32[]{:S(2)}, u32[]{:S(2)}) collective-permute-start(bf16[7,2048]{1,0:T(8,128)(2,1)S(1)} %slice.64), channel_id=1, source_target_pairs={{0,2},{2,4},{4,6},{6,8},{8,10},{10,12},{12,14},{14,16},{16,18},{18... | collective-permute-start | bytes 86024 | tf_op jit(solution)/shard_map/ppermute | solution.py:20
  11.8 6.6 %copy-start.2 = (bf16[256,2048]{1,0:T(8,128)(2,1)S(1)}, bf16[256,2048]{1,0:T(8,128)(2,1)}, u32[]{:S(2)}) copy-start(bf16[256,2048]{1,0:T(8,128)(2,1)} %param.16) | copy-start | bytes 3145732
  13.1 55.2 %all-to-all-start = ((bf16[16,128,256]{2,1,0:T(8,128)(2,1)}), bf16[16,128,256]{2,1,0:T(8,128)(2,1)}, u32[]{:S(2)}, u32[]{:S(2)}) async-start(bf16[16,128,256]{2,1,0:T(8,128)(2,1)} %bitcast.16), calls=%async_computation | async-start | bytes 2097152 | tf_op jit(solution)/shard_map/all_to_all | solution.py:120
  19.7 35.3 %collective-permute-start.3 = (bf16[256,2048]{0,1:T(8,128)(2,1)}, bf16[256,2048]{0,1:T(8,128)(2,1)}, u32[]{:S(2)}, u32[]{:S(2)}) collective-permute-start(bf16[256,2048]{0,1:T(8,128)(2,1)} %copy.55), channel_id=1, source_target_pairs={{0,2},{2,4},{4,6},{6,8},{8,10},{10,12},{12,14},{14,16},{16,18},{18... | collective-permute-start | bytes 3145736 | tf_op jit(solution)/shard_map/ppermute | solution.py:20
  21.8 44.5 %collective-permute-start = (bf16[256,2048]{1,0:T(8,128)(2,1)}, bf16[256,2048]{1,0:T(8,128)(2,1)}, u32[]{:S(2)}, u32[]{:S(2)}) collective-permute-start(bf16[256,2048]{1,0:T(8,128)(2,1)} %param.17), channel_id=1, source_target_pairs={{0,2},{2,4},{4,6},{6,8},{8,10},{10,12},{12,14},{14,16},{16,18},{18... | collective-permute-start | bytes 3145736 | tf_op jit(solution)/shard_map/ppermute | solution.py:20
  55.0 124.6 %collective-permute-start.4 = (bf16[256,2048]{0,1:T(8,128)(2,1)}, bf16[256,2048]{0,1:T(8,128)(2,1)}, u32[]{:S(2)}, u32[]{:S(2)}) collective-permute-start(bf16[256,2048]{0,1:T(8,128)(2,1)} %collective-permute-done.3), channel_id=1, source_target_pairs={{0,2},{2,4},{4,6},{6,8},{8,10},{10,12},{12,14},{14,16},{16,18},{18... | collective-permute-start | bytes 3145736 | tf_op jit(solution)/shard_map/ppermute | solution.py:20
  66.2 137.5 %collective-permute-start.1 = (bf16[256,2048]{1,0:T(8,128)(2,1)}, bf16[256,2048]{1,0:T(8,128)(2,1)}, u32[]{:S(2)}, u32[]{:S(2)}) collective-permute-start(bf16[256,2048]{1,0:T(8,128)(2,1)} %collective-permute-done), channel_id=1, source_target_pairs={{0,2},{2,4},{4,6},{6,8},{8,10},{10,12},{12,14},{14,16},{16,18},{18... | collective-permute-start | bytes 3145736 | tf_op jit(solution)/shard_map/ppermute | solution.py:20
  79.7 10.9 %copy-start.1 = (f32[256,32,128]{2,1,0:T(8,128)S(1)}, f32[256,32,128]{2,1,0:T(8,128)}, u32[]{:S(2)}) copy-start(f32[256,32,128]{2,1,0:T(8,128)} %copy.75) | copy-start | bytes 12582916
  179.6 26.2 %collective-permute-start.5 = (bf16[256,2048]{0,1:T(8,128)(2,1)}, bf16[256,2048]{0,1:T(8,128)(2,1)}, u32[]{:S(2)}, u32[]{:S(2)}) collective-permute-start(bf16[256,2048]{0,1:T(8,128)(2,1)} %collective-permute-done.4), channel_id=1, source_target_pairs={{0,2},{2,4},{4,6},{6,8},{8,10},{10,12},{12,14},{14,16},{16,18},{18... | collective-permute-start | bytes 3145736 | tf_op jit(solution)/shard_map/ppermute | solution.py:20
  197.9 67.6 %all-to-all-start.1 = ((bf16[128,16,256]{2,0,1:T(8,128)(2,1)}), bf16[128,16,256]{2,0,1:T(8,128)(2,1)S(1)}, u32[]{:S(2)}, u32[]{:S(2)}) async-start(bf16[128,16,256]{2,0,1:T(8,128)(2,1)} %copy.71), calls=%async_computation.1 | async-start | bytes 2097152 | tf_op jit(solution)/shard_map/all_to_all | solution.py:124
  203.7 36.5 %collective-permute-start.2 = (bf16[256,2048]{1,0:T(8,128)(2,1)}, bf16[256,2048]{1,0:T(8,128)(2,1)S(1)}, u32[]{:S(2)}, u32[]{:S(2)}) collective-permute-start(bf16[256,2048]{1,0:T(8,128)(2,1)} %collective-permute-done.1), channel_id=1, source_target_pairs={{0,2},{2,4},{4,6},{6,8},{8,10},{10,12},{12,14},{14,16},{16,18},{18... | collective-permute-start | bytes 3145736 | tf_op jit(solution)/shard_map/ppermute | solution.py:20
  267.1 8.5 %copy-start.3 = (f32[2048]{0:T(1024)S(1)}, f32[2048]{0:T(1024)}, u32[]{:S(2)}) copy-start(f32[2048]{0:T(1024)} %param.19) | copy-start | bytes 24580
  267.1 8.5 %copy-start.4 = (f32[2048]{0:T(1024)S(1)}, f32[2048]{0:T(1024)}, u32[]{:S(2)}) copy-start(f32[2048]{0:T(1024)} %param.18) | copy-start | bytes 24580
where the time goes:
time: 283 us; the launch traced here: 279 us
  matrix products  129 us (46%)
  waiting for transfers between devices  55 us (19%)
  other arithmetic  35.2 us (12%)
  local copies, waits for them, and re-layouts  27.5 us (10%)
  starting transfers between devices  26.8 us (9%)
  blocking collectives  4.94 us (2%)
    ppermute x7, waiting for transfers between devices, shifted_2(): return lax.ppermute(block, axis, route)  55 us
    dot_general x1, matrix products, long_conv(): jnp.einsum('ckb,bm->ckm', real_b, cos_two, precision=exact_mode)  16.2 us
    dot_general x1, matrix products, long_conv(): jnp.einsum('ckb,bm->ckm', real_b, sin_two, precision=exact_mode)  15.8 us
    ppermute x7, starting transfers between devices, shifted_2(): return lax.ppermute(block, axis, route)  15.7 us
    dot_general x1, matrix products, long_conv(): jnp.einsum('ckb,bm->ckm', imag_b, sin_two, precision=exact_mode)  15.7 us
    dot_general x1, matrix products, long_conv(): jnp.einsum('ckb,bm->ckm', imag_b, cos_two, precision=exact_mode)  14.1 us
    dot_general x1, matrix products, attend(): jnp.einsum('hqk,khd->qhd', weights, value_heads, preferred_element_type=j...  12.4 us
    dot_general x1, matrix products, long_conv(): real_a = jnp.einsum('cab,ak->ckb', stacked, cos_one, precision=exact_mode)  11 us
  transfers between devices with their start and end apart: 9, of which 4 were waited for; matrix products, arithmetic and copies ran while one was open for 63% of the time, Pallas kernels for 0%

commit v1 on v0

v1 whole, which is shorter than its diff:
```python
import functools
import math

import jax
import jax.numpy as jnp
import ml_dtypes
import numpy as np
from jax import lax
from jax.experimental import pallas as pl
from jax.experimental.pallas import tpu as pltpu
from jax.sharding import PartitionSpec as P

D = 4096
HD = 128
TAPS = 8
SPAN = 3
EDGE = 16
EPS = 1e-05
F32 = jnp.float32
BF16 = jnp.bfloat16
VMEM = pl.BlockSpec(memory_space=pltpu.VMEM)


def params(mib, **more):
    return pltpu.CompilerParams(vmem_limit_bytes=mib * 2**20, **more)


def moved(block, distance):
    count = lax.axis_size("seq")
    return lax.ppermute(block, "seq", [(i, i + distance) for i in range(count - distance)])


def shift_kernel(key_ref, before_ref, value_ref, taps_ref, out_ref, ext_ref):
    count, width = key_ref.shape
    ext_ref[0:EDGE, :] = before_ref[...].astype(F32)
    ext_ref[EDGE:, :] = key_ref[...].astype(F32)
    total = taps_ref[0:1, :] * ext_ref[EDGE : EDGE + count, :]
    for j in range(1, TAPS):
        total = total + taps_ref[j : j + 1, :] * ext_ref[EDGE - j : EDGE - j + count, :]
    product = (total * value_ref[...].astype(F32)).astype(BF16)
    for g in range(width // 128):
        out_ref[g] = product[:, g * 128 : (g + 1) * 128]


def shift_filter(key, before, value, taps):
    count, width = key.shape
    step = min(width, 512)
    return pl.pallas_call(
        shift_kernel,
        grid=(width // step,),
        in_specs=[
            pl.BlockSpec((count, step), lambda g: (0, g)),
            pl.BlockSpec((EDGE, step), lambda g: (0, g)),
            pl.BlockSpec((count, step), lambda g: (0, g)),
            pl.BlockSpec((TAPS, step), lambda g: (0, g)),
        ],
        out_specs=pl.BlockSpec((step // 128, count, 128), lambda g: (g, 0, 0)),
        out_shape=jax.ShapeDtypeStruct((width // 128, count, 128), BF16),
        scratch_shapes=[pltpu.VMEM((count + EDGE, step), F32)],
        compiler_params=params(32),
        name="shift",
    )(key, before, value, taps)


def fft(values, sign):
    n = len(values)
    if n == 1:
        return values
    even = fft(values[0::2], sign)
    odd = fft(values[1::2], sign)
    low, high = [], []
    for k in range(n // 2):
        er, ei = even[k]
        orr, oi = odd[k]
        if k == 0:
            tr, ti = orr, oi
        elif 4 * k == n:
            tr, ti = (-oi, orr) if sign > 0 else (oi, -orr)
        else:
            c = math.cos(2 * math.pi * k / n)
            s = sign * math.sin(2 * math.pi * k / n)
            if 8 * k == n:
                tr, ti = ((orr - oi) * c, (orr + oi) * c) if sign > 0 else ((orr + oi) * c, (oi - orr) * c)
            elif 8 * k == 3 * n:
                h = -c
                tr, ti = ((-orr - oi) * h, (orr - oi) * h) if sign > 0 else ((oi - orr) * h, (-orr - oi) * h)
            else:
                tr, ti = orr * c - oi * s, orr * s + oi * c
        low.append((er + tr, ei + ti))
        high.append((er - tr, ei - ti))
    return low + high


def plan(length):
    return 32 if length <= 8192 else 64


def split(table):
    high = table.astype(ml_dtypes.bfloat16)
    low = (table - high.astype(np.float64)).astype(ml_dtypes.bfloat16)
    return high, low


def tables(length):
    outer = plan(length)
    inner = length // outer
    period = 2 * length
    b = np.arange(inner)
    angle = 2 * np.pi / inner * (np.outer(b, b) % inner)
    c, s = np.cos(angle), np.sin(angle)
    forward = np.block([[c, s], [-s, c]])
    twist = 2 * np.pi / period * np.outer(b, 2 * np.arange(outer) + 0.5)
    return (
        split(forward),
        split(forward.T),
        np.cos(twist).astype(np.float32),
        np.sin(twist).astype(np.float32),
    )


def dot(a, b):
    return jnp.dot(a, b, preferred_element_type=F32)


def dot3(gh_ref, gl_ref, z):
    zh = z.astype(BF16)
    zl = (z - zh.astype(F32)).astype(BF16)
    gh = gh_ref[...]
    return dot(gh, zh) + dot(gh, zl) + dot(gl_ref[...], zh)


def outer_forward(xf_ref, z_ref, c_ref, s_ref, outer):
    inner = c_ref.shape[0]

    def body(i, carry):
        r = pl.multiple_of(i * 8, 8)
        values = []
        for a in range(outer):
            x = xf_ref[pl.ds(pl.multiple_of(a * inner + r, 8), 8), :]
            w = math.pi * a / (2 * outer)
            values.append((x * math.cos(w), x * (-math.sin(w))))
        values = fft(values, -1)
        c, s = c_ref[pl.ds(r, 8), :], s_ref[pl.ds(r, 8), :]
        for k in range(outer):
            zr, zi = values[k]
            ck, sk = c[:, k : k + 1], s[:, k : k + 1]
            z_ref[k, pl.ds(r, 8), :] = zr * ck + zi * sk
            z_ref[k, pl.ds(pl.multiple_of(inner + r, 8), 8), :] = zi * ck - zr * sk
        return carry

    lax.fori_loop(0, inner // 8, body, 0)


def outer_inverse(z_ref, xf_ref, c_ref, s_ref, outer):
    inner = c_ref.shape[0]

    def body(i, carry):
        r = pl.multiple_of(i * 8, 8)
        c, s = c_ref[pl.ds(r, 8), :], s_ref[pl.ds(r, 8), :]
        values = []
        for k in range(outer):
            zr = z_ref[k, pl.ds(r, 8), :]
            zi = z_ref[k, pl.ds(pl.multiple_of(inner + r, 8), 8), :]
            ck, sk = c[:, k : k + 1], s[:, k : k + 1]
            values.append((zr * ck - zi * sk, zi * ck + zr * sk))
        values = fft(values, 1)
        for a in range(outer):
            w = math.pi * a / (2 * outer)
            scale = 1.0 / (outer * inner)
            y = values[a][0] * (scale * math.cos(w)) - values[a][1] * (scale * math.sin(w))
            xf_ref[pl.ds(pl.multiple_of(a * inner + r, 8), 8), :] = y
        return carry

    lax.fori_loop(0, inner // 8, body, 0)


def kernel_spectrum_kernel(outer, ker_ref, gh_ref, gl_ref, c_ref, s_ref, out_ref, xf_ref, z_ref):
    inner = c_ref.shape[0]
    for a in range(outer):
        xf_ref[a * inner : (a + 1) * inner, :] = ker_ref[:, a * inner : (a + 1) * inner].T
    outer_forward(xf_ref, z_ref, c_ref, s_ref, outer)

    def body(j, carry):
        z = jnp.concatenate([z_ref[2 * j], z_ref[2 * j + 1]], axis=1)
        h = dot3(gh_ref, gl_ref, z)
        number = h.shape[1] // 2
        out_ref[2 * j] = h[:, :number]
        out_ref[2 * j + 1] = h[:, number:]
        return carry

    lax.fori_loop(0, outer // 2, body, 0)


def conv_kernel_body(outer, sig_ref, spec_ref, gh_ref, gl_ref, ih_ref, il_ref, c_ref, s_ref, out_ref, xf_ref, z_ref):
    inner = c_ref.shape[0]
    xf_ref[...] = sig_ref[...].astype(F32)
    outer_forward(xf_ref, z_ref, c_ref, s_ref, outer)

    def body(j, carry):
        z = jnp.concatenate([z_ref[2 * j], z_ref[2 * j + 1]], axis=1)
        h = jnp.concatenate([spec_ref[2 * j], spec_ref[2 * j + 1]], axis=1)
        f = dot3(gh_ref, gl_ref, z)
        fr, fi = f[:inner], f[inner:]
        hr, hi = h[:inner], h[inner:]
        p = jnp.concatenate([fr * hr - fi * hi, fr * hi + fi * hr], axis=0)
        w = dot3(ih_ref, il_ref, p)
        number = w.shape[1] // 2
        z_ref[2 * j] = w[:, :number]
        z_ref[2 * j + 1] = w[:, number:]
        return carry

    lax.fori_loop(0, outer // 2, body, 0)
    outer_inverse(z_ref, xf_ref, c_ref, s_ref, outer)
    out_ref[...] = xf_ref[...].astype(BF16)


def kernel_spectrum(kernel):
    number, length = kernel.shape
    outer = plan(length)
    inner = length // outer
    (gh, gl), _, c, s = tables(length)
    return pl.pallas_call(
        functools.partial(kernel_spectrum_kernel, outer),
        in_specs=[VMEM] * 5,
        out_specs=VMEM,
        out_shape=jax.ShapeDtypeStruct((outer, 2 * inner, number), F32),
        scratch_shapes=[
            pltpu.VMEM((length, number), F32),
            pltpu.VMEM((outer, 2 * inner, number), F32),
        ],
        compiler_params=params(60),
        cost_estimate=pl.CostEstimate(flops=6 * 10**9, bytes_accessed=7 * 2**20, transcendentals=0),
        name="kernel_spectrum",
    )(kernel, gh, gl, c, s)


def long_conv(signal, spectrum):
    length, number = signal.shape
    outer = plan(length)
    inner = length // outer
    (gh, gl), (ih, il), c, s = tables(length)
    return pl.pallas_call(
        functools.partial(conv_kernel_body, outer),
        in_specs=[VMEM] * 8,
        out_specs=VMEM,
        out_shape=jax.ShapeDtypeStruct((length, number), BF16),
        scratch_shapes=[
            pltpu.VMEM((length, number), F32),
            pltpu.VMEM((outer, 2 * inner, number), F32),
        ],
        compiler_params=params(60),
        cost_estimate=pl.CostEstimate(flops=12 * 10**9, bytes_accessed=7 * 2**20, transcendentals=0),
        name="long_conv",
    )(signal, spectrum, gh, gl, ih, il, c, s)


def row_sums(square):
    ones = jnp.ones((8, square.shape[1]), F32)
    return lax.dot_general(
        ones, square, (((1,), (1,)), ((), ())), precision=lax.Precision.HIGHEST, preferred_element_type=F32
    )


def attention_kernel(*refs):
    query_ref = refs[0]
    keys = refs[1 : 2 + SPAN]
    values = refs[2 + SPAN : 3 + 2 * SPAN]
    out_ref, sum_ref, acc_ref = refs[3 + 2 * SPAN :]
    count, width = query_ref.shape
    step = pl.program_id(0)
    me = lax.axis_index("seq")

    @pl.when(step == 0)
    def _():
        acc_ref[...] = jnp.zeros_like(acc_ref)

    row = lax.broadcasted_iota(jnp.int32, (count, count), 0)
    col = lax.broadcasted_iota(jnp.int32, (count, count), 1)
    causal = col <= row
    scale = math.log2(math.e) / math.sqrt(HD)
    for h in range(width // HD):
        lanes = slice(h * HD, (h + 1) * HD)
        q = query_ref[:, lanes]
        scores = []
        for j in range(SPAN + 1):
            s = lax.dot_general(q, keys[j][:, lanes], (((1,), (1,)), ((), ())), preferred_element_type=F32)
            if j == 0:
                s = jnp.where(causal, s, -1e30)
            else:
                s = jnp.where(me >= j, s, -1e30)
            scores.append(s)
        peak = functools.reduce(jnp.maximum, scores)
        top = jnp.max(peak, axis=1, keepdims=True)
        numer = jnp.zeros((count, HD), F32)
        total = jnp.zeros((count, count), F32)
        for j in range(SPAN + 1):
            p = jnp.exp2((scores[j] - top) * scale)
            total = total + p
            numer = numer + dot(p.astype(BF16), values[j][:, lanes])
        o = numer / jnp.sum(total, axis=1, keepdims=True)
        out_ref[:, lanes] = o
        acc_ref[...] += o * o

    @pl.when(step == pl.num_programs(0) - 1)
    def _():
        sum_ref[...] = row_sums(acc_ref[...])


def attention(query, keys, values):
    count, width = query.shape
    step = min(width, 256)
    block = pl.BlockSpec((count, step), lambda g: (0, g))
    return pl.pallas_call(
        attention_kernel,
        grid=(width // step,),
        in_specs=[block] * (3 + 2 * SPAN),
        out_specs=[block, pl.BlockSpec((8, count), lambda g: (0, 0))],
        out_shape=[
            jax.ShapeDtypeStruct((count, width), F32),
            jax.ShapeDtypeStruct((8, count), F32),
        ],
        scratch_shapes=[pltpu.VMEM((count, HD), F32)],
        compiler_params=params(40),
        cost_estimate=pl.CostEstimate(flops=5 * 10**9, bytes_accessed=11 * 2**20, transcendentals=4 * 10**6),
        name="attention",
    )(query, *keys, *values)


def mixer_sums_kernel(query_ref, filtered_ref, sum_ref):
    groups, count, lanes = filtered_ref.shape
    acc = jnp.zeros((count, lanes), F32)
    for g in range(groups):
        m = query_ref[:, g * lanes : (g + 1) * lanes].astype(F32) * filtered_ref[g].astype(F32)
        acc = acc + m * m
    sum_ref[...] = row_sums(acc)


def mixer_sums(query, filtered):
    return pl.pallas_call(
        mixer_sums_kernel,
        in_specs=[VMEM] * 2,
        out_specs=VMEM,
        out_shape=jax.ShapeDtypeStruct((8, query.shape[0]), F32),
        compiler_params=params(32),
        name="mixer_sums",
    )(query, filtered)


def join_kernel(attn_ref, query_ref, filtered_ref, asum_ref, msum_ref, beta_a_ref, beta_m_ref, out_ref):
    lanes = filtered_ref.shape[2]
    a_scale = (0.5 * lax.rsqrt(asum_ref[...] / D + EPS)).T[:, 0:1]
    m_scale = (0.5 * lax.rsqrt(msum_ref[...] / D + EPS)).T[:, 0:1]
    for g in range(filtered_ref.shape[0]):
        at = slice(g * lanes, (g + 1) * lanes)
        m = query_ref[:, at].astype(F32) * filtered_ref[g].astype(F32)
        y = beta_a_ref[:, at] * (attn_ref[:, at] * a_scale) + beta_m_ref[:, at] * (m * m_scale)
        out_ref[:, at] = y.astype(BF16)


def join(attn, query, filtered, asum, msum, beta_a, beta_m):
    count, width = query.shape
    step = min(width, 512)
    block = pl.BlockSpec((count, step), lambda g: (0, g))
    sums = pl.BlockSpec((8, count), lambda g: (0, 0))
    beta = pl.BlockSpec((1, step), lambda g: (0, g))
    return pl.pallas_call(
        join_kernel,
        grid=(width // step,),
        in_specs=[block, block, pl.BlockSpec((step // 128, count, 128), lambda g: (g, 0, 0)), sums, sums, beta, beta],
        out_specs=block,
        out_shape=jax.ShapeDtypeStruct((count, width), BF16),
        compiler_params=params(32),
        name="join",
    )(attn, query, filtered, asum, msum, beta_a[None, :], beta_m[None, :])


def on_device(
    mixer_query,
    mixer_key,
    mixer_value,
    shift_taps,
    conv_kernel,
    heads_query,
    heads_key,
    heads_value,
    beta_attention,
    beta_mixer,
):
    count, width = mixer_key.shape
    devices = lax.axis_size("seq")
    number, length = conv_kernel.shape
    before = moved(mixer_key[count - EDGE :], 1)
    ssm_input = shift_filter(mixer_key, before, mixer_value, shift_taps)
    if number != 128:
        ssm_input = jnp.transpose(ssm_input, (1, 0, 2)).reshape(count, devices, number)
        ssm_input = jnp.transpose(ssm_input, (1, 0, 2))
    signal = lax.all_to_all(ssm_input, "seq", split_axis=0, concat_axis=0, tiled=True)
    spectrum = kernel_spectrum(conv_kernel)
    keys = [heads_key] + [moved(heads_key, j) for j in range(1, SPAN + 1)]
    values = [heads_value] + [moved(heads_value, j) for j in range(1, SPAN + 1)]
    filtered = long_conv(signal.reshape(length, number), spectrum)
    filtered = filtered.reshape(devices, count, number)
    returned = lax.all_to_all(filtered, "seq", split_axis=0, concat_axis=0, tiled=True)
    if number != 128:
        returned = jnp.transpose(returned, (1, 0, 2)).reshape(count, width // 128, 128)
        returned = jnp.transpose(returned, (1, 0, 2))
    attn, asum = attention(heads_query, keys, values)
    msum = mixer_sums(mixer_query, returned)
    asum = lax.psum(asum, "head")
    msum = lax.psum(msum, "head")
    return join(attn, mixer_query, returned, asum, msum, beta_attention, beta_mixer)


def solution(mesh):
    return jax.shard_map(
        on_device,
        mesh=mesh,
        in_specs=(
            P("seq", "head"),
            P("seq", "head"),
            P("seq", "head"),
            P(None, "head"),
            P(("head", "seq"), None),
            P("seq", "head"),
            P("seq", "head"),
            P("seq", "head"),
            P("head"),
            P("head"),
        ),
        out_specs=P("seq", "head"),
        check_vma=False,
    )
```

time: 283 us -> 226 us (0.80)
  the two profiles are of different devices: /device:TPU:16 before, /device:TPU:20 now
where the time goes in v1:
time: 226 us
  waiting for transfers between devices  126 us (56%)
  Pallas kernels  52.4 us (23%)
  starting transfers between devices  29.4 us (13%)
  local copies, waits for them, and re-layouts  9.25 us (4%)
  blocking collectives  8.1 us (4%)
    ppermute x7, waiting for transfers between devices, moved(): lax.ppermute(block, 'seq', [(i, i + distance) for i in range(count - dist...  116 us
    pallas_call x1, Pallas kernels, long_conv(): pl.pallas_call(functools.partial(conv_kernel_body, outer), in_specs=[VMEM...  21.8 us
    ppermute x7, starting transfers between devices, moved(): lax.ppermute(block, 'seq', [(i, i + distance) for i in range(count - dist...  16.6 us
    pallas_call x1, Pallas kernels, kernel_spectrum(): pl.pallas_call(functools.partial(kernel_spectrum_kernel, outer), in_specs...  11.5 us
    pallas_call x1, Pallas kernels, attention(): pl.pallas_call(attention_kernel, grid=(width // step,), in_specs=[block]...  11.5 us
    all_to_all x1, waiting for transfers between devices, on_device(): lax.all_to_all(ssm_input, 'seq', split_axis=0, concat_axis=0, tiled=True)  9.83 us
    unnamed x22, local copies, waits for them, and re-layouts  8.41 us
    psum x1, blocking collectives, on_device(): asum = lax.psum(asum, 'head')  8.1 us
  transfers between devices with their start and end apart: 9, of which 6 were waited for; matrix products, arithmetic and copies ran while one was open for 0% of the time, Pallas kernels for 20%

profile of v1, /device:TPU:20, one launch (start us, length us, event | category | flops | bytes accessed | tf_op | source)
XLA Modules:
  0.0 225.6 jit_solution(17722386212907282000)
XLA Ops:
  0.0 0.8 slice.3
  0.8 1.9 collective-permute-start.6
  2.8 3.7 %collective-permute-done.6.before_ref = bf16[16,2048]{1,0:T(8,128)(2,1)S(1)} collective-permute-done((bf16[16,2048]{1,0:T(8,128)(2,1)S(1)}, bf16[16,2048]{1,0:T(8,128)(2,1)S(1)}, u32[]{:S(2)}, u32[]{:S(2)}) %collective-permute-start.6) | collective-permute-done | bytes 65568 | tf_op jit(solution)/shard_map/ppermute | solution.py:30
  6.4 1.2 copy-done.3
  7.6 1.2 copy-done.4
  8.9 0.8 copy-done.5
  9.7 4.6 %shift.1 = bf16[16,256,128]{2,1,0:T(8,128)(2,1)} custom-call(bf16[256,2048]{1,0:T(8,128)(2,1)S(1)} %copy-done.3, bf16[16,2048]{1,0:T(8,128)(2,1)S(1)} %collective-permute-done.6.before_ref, bf16[256,2048]{1,0:T(8,128)(2,1)S(1)} %copy-done.4, f32[8,2048]{1,0:T(8,128)S(1)} %copy-done.5), custom_call_target="tpu_custom_call" | custom-call | tf_op jit(solution)/shard_map/shift/pallas_call | solution.py:48
  14.3 6.1 %all-to-all-start = ((bf16[16,256,128]{2,1,0:T(8,128)(2,1)}), bf16[16,256,128]{2,1,0:T(8,128)(2,1)S(1)}, u32[]{:S(2)}, u32[]{:S(2)}) async-start(bf16[16,256,128]{2,1,0:T(8,128)(2,1)} %shift.1), calls=%async_computation | async-start | bytes 2097152 | tf_op jit(solution)/shard_map/all_to_all | solution.py:397
  20.5 2.0 collective-permute-start
  22.5 11.5 %kernel_spectrum.1.spec_ref = f32[32,256,128]{2,1,0:T(8,128)} custom-call(f32[128,4096]{1,0:T(8,128)} %ker_ref.1, bf16[256,256]{1,0:T(8,128)(2,1)} %constant.12.clone.gh_ref, bf16[256,256]{1,0:T(8,128)(2,1)} %constant.13.clone.gl_ref, f32[128,32]{1,0:T(8,128)} %constant.14.clone.c_ref, f32[128,32]{1,0:T(8,128)} %constant.15.clone.s_ref), custom_call_target="tpu_custom_call" | custom-call | flops 6000000000 | bytes 7340032 | tf_op jit(solution)/shard_map/kernel_spectrum/pallas_call | solution.py:222
  34.0 9.8 %all-to-all-done = bf16[16,256,128]{2,1,0:T(8,128)(2,1)S(1)} async-done(((bf16[16,256,128]{2,1,0:T(8,128)(2,1)}), bf16[16,256,128]{2,1,0:T(8,128)(2,1)S(1)}, u32[]{:S(2)}, u32[]{:S(2)}) %all-to-all-start) | async-done | bytes 1048608 | tf_op jit(solution)/shard_map/all_to_all | solution.py:397
  43.9 1.0 copy-done.10
  44.8 21.8 %long_conv.1 = bf16[4096,128]{1,0:T(8,128)(2,1)} custom-call(bf16[4096,128]{1,0:T(8,128)(2,1)} %bitcast.7, f32[32,256,128]{2,1,0:T(8,128)} %kernel_spectrum.1.spec_ref, bf16[256,256]{1,0:T(8,128)(2,1)} %constant.12.clone.gh_ref, bf16[256,256]{1,0:T(8,128)(2,1)} %constant.13.clone.gl_ref, bf16[256,256]{1,0:T(8,128)(2,1)} %constant.16.clone.ih_ref, ...), custom_call_target="tpu_custom_call" | custom-call | flops 12000000000 | bytes 7340032 | tf_op jit(solution)/shard_map/long_conv/pallas_call | solution.py:242
  66.6 6.7 %all-to-all-start.1 = ((bf16[16,256,128]{2,1,0:T(8,128)(2,1)}), bf16[16,256,128]{2,1,0:T(8,128)(2,1)S(1)}, u32[]{:S(2)}, u32[]{:S(2)}) async-start(bf16[16,256,128]{2,1,0:T(8,128)(2,1)} %bitcast.6), calls=%async_computation.1 | async-start | bytes 2097152 | tf_op jit(solution)/shard_map/all_to_all | solution.py:403
  73.3 3.5 %collective-permute-start.1 = (bf16[256,2048]{1,0:T(8,128)(2,1)}, bf16[256,2048]{1,0:T(8,128)(2,1)S(1)}, u32[]{:S(2)}, u32[]{:S(2)}) collective-permute-start(bf16[256,2048]{1,0:T(8,128)(2,1)} %refs_1_.1), channel_id=1, source_target_pairs={{0,4},{2,6},{4,8},{6,10},{8,12},{10,14},{12,16},{14,18},{16,20},{1... | collective-permute-start | bytes 3145736 | tf_op jit(solution)/shard_map/ppermute | solution.py:30
  76.8 2.8 %collective-permute-start.2 = (bf16[256,2048]{1,0:T(8,128)(2,1)}, bf16[256,2048]{1,0:T(8,128)(2,1)S(1)}, u32[]{:S(2)}, u32[]{:S(2)}) collective-permute-start(bf16[256,2048]{1,0:T(8,128)(2,1)} %refs_1_.1), channel_id=1, source_target_pairs={{0,6},{2,8},{4,10},{6,12},{8,14},{10,16},{12,18},{14,20},{16,22},{... | collective-permute-start | bytes 3145736 | tf_op jit(solution)/shard_map/ppermute | solution.py:30
  79.7 1.9 collective-permute-start.3
  81.6 2.4 %collective-permute-start.4 = (bf16[256,2048]{1,0:T(8,128)(2,1)}, bf16[256,2048]{1,0:T(8,128)(2,1)S(1)}, u32[]{:S(2)}, u32[]{:S(2)}) collective-permute-start(bf16[256,2048]{1,0:T(8,128)(2,1)} %refs_5_.1), channel_id=1, source_target_pairs={{0,4},{2,6},{4,8},{6,10},{8,12},{10,14},{12,16},{14,18},{16,20},{1... | collective-permute-start | bytes 3145736 | tf_op jit(solution)/shard_map/ppermute | solution.py:30
  84.1 0.0 collective-permute-done.refs_2_
  84.1 1.9 collective-permute-start.5
  86.0 27.9 %collective-permute-done.1.refs_3_ = bf16[256,2048]{1,0:T(8,128)(2,1)S(1)} collective-permute-done((bf16[256,2048]{1,0:T(8,128)(2,1)}, bf16[256,2048]{1,0:T(8,128)(2,1)S(1)}, u32[]{:S(2)}, u32[]{:S(2)}) %collective-permute-start.1) | collective-permute-done | bytes 1048608 | tf_op jit(solution)/shard_map/ppermute | solution.py:30
  113.9 28.2 %collective-permute-done.2.refs_4_ = bf16[256,2048]{1,0:T(8,128)(2,1)S(1)} collective-permute-done((bf16[256,2048]{1,0:T(8,128)(2,1)}, bf16[256,2048]{1,0:T(8,128)(2,1)S(1)}, u32[]{:S(2)}, u32[]{:S(2)}) %collective-permute-start.2) | collective-permute-done | bytes 1048608 | tf_op jit(solution)/shard_map/ppermute | solution.py:30
  142.1 0.0 collective-permute-done.3.refs_6_
  142.1 16.8 %collective-permute-done.4.refs_7_ = bf16[256,2048]{1,0:T(8,128)(2,1)S(1)} collective-permute-done((bf16[256,2048]{1,0:T(8,128)(2,1)}, bf16[256,2048]{1,0:T(8,128)(2,1)S(1)}, u32[]{:S(2)}, u32[]{:S(2)}) %collective-permute-start.4) | collective-permute-done | bytes 1048608 | tf_op jit(solution)/shard_map/ppermute | solution.py:30
  158.9 39.9 %collective-permute-done.5.refs_8_ = bf16[256,2048]{1,0:T(8,128)(2,1)S(1)} collective-permute-done((bf16[256,2048]{1,0:T(8,128)(2,1)}, bf16[256,2048]{1,0:T(8,128)(2,1)S(1)}, u32[]{:S(2)}, u32[]{:S(2)}) %collective-permute-start.5) | collective-permute-done | bytes 1048608 | tf_op jit(solution)/shard_map/ppermute | solution.py:30
  198.8 1.2 copy-done.9
  200.0 11.5 %attention.1 = (f32[256,2048]{1,0:T(8,128)S(1)}, f32[8,256]{1,0:T(8,128)S(1)}) custom-call(bf16[256,2048]{1,0:T(8,128)(2,1)S(1)} %copy-done.8, bf16[256,2048]{1,0:T(8,128)(2,1)} %refs_1_.1, bf16[256,2048]{1,0:T(8,128)(2,1)} %collective-permute-done.refs_2_, bf16[256,2048]{1,0:T(8,128)(2,1)S(1)} %collective-permute-done.1.refs_3_, ...), custom_call_target="tpu_custom_call" | custom-call | flops 5000000000 | bytes 11534336 | tf_op jit(solution)/shard_map/attention/pallas_call | solution.py:313
  211.5 1.3 copy-done.1
  212.8 0.5 mixer_sums.1
  213.3 8.1 %all-reduce = (f32[8,256]{1,0:T(8,128)S(1)}, f32[8,256]{1,0:T(8,128)S(1)}) all-reduce(f32[8,256]{1,0:T(8,128)S(1)} %get-tuple-element.8, f32[8,256]{1,0:T(8,128)S(1)} %mixer_sums.1), channel_id=1, replica_groups=mesh['seq'=16,'head'=2] {'head'}, use_global_device_ids=true, to_apply=%region_0.0 | all-reduce | flops 4096 | bytes 32768 | tf_op jit(solution)/shard_map/psum | solution.py:409
  221.4 1.6 copy-done.2
  223.0 2.6 %join.1 = bf16[256,2048]{1,0:T(8,128)(2,1)} custom-call(f32[256,2048]{1,0:T(8,128)S(1)} %copy-done.2, bf16[256,2048]{1,0:T(8,128)(2,1)S(1)} %copy-done, bf16[16,256,128]{2,1,0:T(8,128)(2,1)S(1)} %all-to-all-done.1.filtered_ref, f32[8,256]{1,0:T(8,128)S(1)} %get-tuple-element.9.asum_ref, f32[8,256]{1,0:T(8,128)S(1)} %get-tuple-element.10.msum_ref, ...), custom_call_target="tpu_custom_call" | custom-call | tf_op jit(solution)/shard_map/join/pallas_call | solution.py:366
  (16 shorter events, 0.0 us)
Async XLA Ops:
  0.8 5.6 %collective-permute-start.6 = (bf16[16,2048]{1,0:T(8,128)(2,1)S(1)}, bf16[16,2048]{1,0:T(8,128)(2,1)S(1)}, u32[]{:S(2)}, u32[]{:S(2)}) collective-permute-start(bf16[16,2048]{1,0:T(8,128)(2,1)S(1)} %slice.3), channel_id=1, source_target_pairs={{0,2},{2,4},{4,6},{6,8},{8,10},{10,12},{12,14},{14,16},{16,18},{18... | collective-permute-start | bytes 196616 | tf_op jit(solution)/shard_map/ppermute | solution.py:30
  6.4 1.2 copy-start.3
  7.6 1.2 copy-start.4
  8.9 0.8 copy-start.5
  14.3 29.5 %all-to-all-start = ((bf16[16,256,128]{2,1,0:T(8,128)(2,1)}), bf16[16,256,128]{2,1,0:T(8,128)(2,1)S(1)}, u32[]{:S(2)}, u32[]{:S(2)}) async-start(bf16[16,256,128]{2,1,0:T(8,128)(2,1)} %shift.1), calls=%async_computation | async-start | bytes 2097152 | tf_op jit(solution)/shard_map/all_to_all | solution.py:397
  20.5 63.6 %collective-permute-start = (bf16[256,2048]{1,0:T(8,128)(2,1)}, bf16[256,2048]{1,0:T(8,128)(2,1)}, u32[]{:S(2)}, u32[]{:S(2)}) collective-permute-start(bf16[256,2048]{1,0:T(8,128)(2,1)} %refs_1_.1), channel_id=1, source_target_pairs={{0,2},{2,4},{4,6},{6,8},{8,10},{10,12},{12,14},{14,16},{16,18},{18... | collective-permute-start | bytes 3145736 | tf_op jit(solution)/shard_map/ppermute | solution.py:30
  43.9 1.0 copy-start.10
  66.6 132.2 %copy-start.8 = (bf16[256,2048]{1,0:T(8,128)(2,1)S(1)}, bf16[256,2048]{1,0:T(8,128)(2,1)}, u32[]{:S(2)}) copy-start(bf16[256,2048]{1,0:T(8,128)(2,1)} %refs_0_.1) | copy-start | bytes 3145732
  66.6 146.2 %all-to-all-start.1 = ((bf16[16,256,128]{2,1,0:T(8,128)(2,1)}), bf16[16,256,128]{2,1,0:T(8,128)(2,1)S(1)}, u32[]{:S(2)}, u32[]{:S(2)}) async-start(bf16[16,256,128]{2,1,0:T(8,128)(2,1)} %bitcast.6), calls=%async_computation.1 | async-start | bytes 2097152 | tf_op jit(solution)/shard_map/all_to_all | solution.py:403
  73.3 139.5 %copy-start = (bf16[256,2048]{1,0:T(8,128)(2,1)S(1)}, bf16[256,2048]{1,0:T(8,128)(2,1)}, u32[]{:S(2)}) copy-start(bf16[256,2048]{1,0:T(8,128)(2,1)} %query_ref.3) | copy-start | bytes 3145732
  73.3 40.6 %collective-permute-start.1 = (bf16[256,2048]{1,0:T(8,128)(2,1)}, bf16[256,2048]{1,0:T(8,128)(2,1)S(1)}, u32[]{:S(2)}, u32[]{:S(2)}) collective-permute-start(bf16[256,2048]{1,0:T(8,128)(2,1)} %refs_1_.1), channel_id=1, source_target_pairs={{0,4},{2,6},{4,8},{6,10},{8,12},{10,14},{12,16},{14,18},{16,20},{1... | collective-permute-start | bytes 3145736 | tf_op jit(solution)/shard_map/ppermute | solution.py:30
  76.8 65.3 %collective-permute-start.2 = (bf16[256,2048]{1,0:T(8,128)(2,1)}, bf16[256,2048]{1,0:T(8,128)(2,1)S(1)}, u32[]{:S(2)}, u32[]{:S(2)}) collective-permute-start(bf16[256,2048]{1,0:T(8,128)(2,1)} %refs_1_.1), channel_id=1, source_target_pairs={{0,6},{2,8},{4,10},{6,12},{8,14},{10,16},{12,18},{14,20},{16,22},{... | collective-permute-start | bytes 3145736 | tf_op jit(solution)/shard_map/ppermute | solution.py:30
  79.7 62.4 %collective-permute-start.3 = (bf16[256,2048]{1,0:T(8,128)(2,1)}, bf16[256,2048]{1,0:T(8,128)(2,1)S(1)}, u32[]{:S(2)}, u32[]{:S(2)}) collective-permute-start(bf16[256,2048]{1,0:T(8,128)(2,1)} %refs_5_.1), channel_id=1, source_target_pairs={{0,2},{2,4},{4,6},{6,8},{8,10},{10,12},{12,14},{14,16},{16,18},{18... | collective-permute-start | bytes 3145736 | tf_op jit(solution)/shard_map/ppermute | solution.py:30
  81.6 77.3 %collective-permute-start.4 = (bf16[256,2048]{1,0:T(8,128)(2,1)}, bf16[256,2048]{1,0:T(8,128)(2,1)S(1)}, u32[]{:S(2)}, u32[]{:S(2)}) collective-permute-start(bf16[256,2048]{1,0:T(8,128)(2,1)} %refs_5_.1), channel_id=1, source_target_pairs={{0,4},{2,6},{4,8},{6,10},{8,12},{10,14},{12,16},{14,18},{16,20},{1... | collective-permute-start | bytes 3145736 | tf_op jit(solution)/shard_map/ppermute | solution.py:30
  84.1 114.7 %collective-permute-start.5 = (bf16[256,2048]{1,0:T(8,128)(2,1)}, bf16[256,2048]{1,0:T(8,128)(2,1)S(1)}, u32[]{:S(2)}, u32[]{:S(2)}) collective-permute-start(bf16[256,2048]{1,0:T(8,128)(2,1)} %refs_5_.1), channel_id=1, source_target_pairs={{0,6},{2,8},{4,10},{6,12},{8,14},{10,16},{12,18},{14,20},{16,22},{... | collective-permute-start | bytes 3145736 | tf_op jit(solution)/shard_map/ppermute | solution.py:30
  198.8 1.2 copy-start.9
  211.5 1.3 copy-start.1
  212.8 8.6 %copy-start.6 = (f32[2048]{0:T(1024)S(1)}, f32[2048]{0:T(1024)}, u32[]{:S(2)}) copy-start(f32[2048]{0:T(1024)} %param.28) | copy-start | bytes 24580
  212.8 8.6 %copy-start.7 = (f32[2048]{0:T(1024)S(1)}, f32[2048]{0:T(1024)}, u32[]{:S(2)}) copy-start(f32[2048]{0:T(1024)} %param.29) | copy-start | bytes 24580
  221.4 1.6 copy-start.2

commit v2 on v1

--- a/solution.py
+++ b/solution.py
@@ -28,6 +28,19 @@
 def moved(block, distance):
     count = lax.axis_size("seq")
     return lax.ppermute(block, "seq", [(i, i + distance) for i in range(count - distance)])
+
+
+def routed(block, pairs):
+    count = lax.axis_size("seq")
+    return lax.ppermute(block, "seq", [(i, j) for i, j in pairs if 0 <= j < count])
+
+
+def earlier(block):
+    ids = range(lax.axis_size("seq"))
+    two = routed(block, [(i, i + 2) for i in ids])
+    cross = routed(block, [(i, i + 1 + 2 * (i % 2)) for i in ids])
+    swapped = routed(two, [(i, i + 1 - 2 * (i % 2)) for i in ids])
+    return [two, swapped, cross]
 
 
 def shift_kernel(key_ref, before_ref, value_ref, taps_ref, out_ref, ext_ref):
@@ -57,7 +70,7 @@
         out_specs=pl.BlockSpec((step // 128, count, 128), lambda g: (g, 0, 0)),
         out_shape=jax.ShapeDtypeStruct((width // 128, count, 128), BF16),
         scratch_shapes=[pltpu.VMEM((count + EDGE, step), F32)],
-        compiler_params=params(32),
+        compiler_params=params(60),
         name="shift",
     )(key, before, value, taps)
 
@@ -191,7 +204,9 @@
     lax.fori_loop(0, outer // 2, body, 0)
 
 
-def conv_kernel_body(outer, sig_ref, spec_ref, gh_ref, gl_ref, ih_ref, il_ref, c_ref, s_ref, out_ref, xf_ref, z_ref):
+def conv_kernel_body(outer, *refs):
+    sig_ref, spec_ref, gh_ref, gl_ref, ih_ref, il_ref, c_ref, s_ref = refs[:8]
+    out_ref, xf_ref, z_ref = refs[-3:]
     inner = c_ref.shape[0]
     xf_ref[...] = sig_ref[...].astype(F32)
     outer_forward(xf_ref, z_ref, c_ref, s_ref, outer)
@@ -234,14 +249,14 @@
     )(kernel, gh, gl, c, s)
 
 
-def long_conv(signal, spectrum):
+def long_conv(signal, spectrum, after):
     length, number = signal.shape
     outer = plan(length)
     inner = length // outer
     (gh, gl), (ih, il), c, s = tables(length)
     return pl.pallas_call(
         functools.partial(conv_kernel_body, outer),
-        in_specs=[VMEM] * 8,
+        in_specs=[VMEM] * 8 + [pl.BlockSpec(memory_space=pl.ANY)] * len(after),
         out_specs=VMEM,
         out_shape=jax.ShapeDtypeStruct((length, number), BF16),
         scratch_shapes=[
@@ -251,7 +266,7 @@
         compiler_params=params(60),
         cost_estimate=pl.CostEstimate(flops=12 * 10**9, bytes_accessed=7 * 2**20, transcendentals=0),
         name="long_conv",
-    )(signal, spectrum, gh, gl, ih, il, c, s)
+    )(signal, spectrum, gh, gl, ih, il, c, s, *after)
 
 
 def row_sums(square):
@@ -269,6 +284,8 @@
     count, width = query_ref.shape
     step = pl.program_id(0)
     me = lax.axis_index("seq")
+    odd = lax.rem(me, 2)
+    back = [0, 2, 1 + 2 * odd, 3 - 2 * odd]
 
     @pl.when(step == 0)
     def _():
@@ -287,7 +304,7 @@
             if j == 0:
                 s = jnp.where(causal, s, -1e30)
             else:
-                s = jnp.where(me >= j, s, -1e30)
+                s = jnp.where(me >= back[j], s, -1e30)
             scores.append(s)
         peak = functools.reduce(jnp.maximum, scores)
         top = jnp.max(peak, axis=1, keepdims=True)
@@ -320,7 +337,7 @@
             jax.ShapeDtypeStruct((8, count), F32),
         ],
         scratch_shapes=[pltpu.VMEM((count, HD), F32)],
-        compiler_params=params(40),
+        compiler_params=params(60),
         cost_estimate=pl.CostEstimate(flops=5 * 10**9, bytes_accessed=11 * 2**20, transcendentals=4 * 10**6),
         name="attention",
     )(query, *keys, *values)
@@ -341,7 +358,7 @@
         in_specs=[VMEM] * 2,
         out_specs=VMEM,
         out_shape=jax.ShapeDtypeStruct((8, query.shape[0]), F32),
-        compiler_params=params(32),
+        compiler_params=params(60),
         name="mixer_sums",
     )(query, filtered)
 
@@ -369,7 +386,7 @@
         in_specs=[block, block, pl.BlockSpec((step // 128, count, 128), lambda g: (g, 0, 0)), sums, sums, beta, beta],
         out_specs=block,
         out_shape=jax.ShapeDtypeStruct((count, width), BF16),
-        compiler_params=params(32),
+        compiler_params=params(60),
         name="join",
     )(attn, query, filtered, asum, msum, beta_a[None, :], beta_m[None, :])
 
@@ -390,21 +407,23 @@
     devices = lax.axis_size("seq")
     number, length = conv_kernel.shape
     before = moved(mixer_key[count - EDGE :], 1)
+    before, heads_key, heads_value = lax.optimization_barrier((before, heads_key, heads_value))
     ssm_input = shift_filter(mixer_key, before, mixer_value, shift_taps)
     if number != 128:
         ssm_input = jnp.transpose(ssm_input, (1, 0, 2)).reshape(count, devices, number)
         ssm_input = jnp.transpose(ssm_input, (1, 0, 2))
     signal = lax.all_to_all(ssm_input, "seq", split_axis=0, concat_axis=0, tiled=True)
     spectrum = kernel_spectrum(conv_kernel)
-    keys = [heads_key] + [moved(heads_key, j) for j in range(1, SPAN + 1)]
-    values = [heads_value] + [moved(heads_value, j) for j in range(1, SPAN + 1)]
-    filtered = long_conv(signal.reshape(length, number), spectrum)
+    keys = earlier(heads_key)
+    values = earlier(heads_value)
+    filtered = long_conv(signal.reshape(length, number), spectrum, keys)
+    filtered, *values = lax.optimization_barrier((filtered, *values))
     filtered = filtered.reshape(devices, count, number)
     returned = lax.all_to_all(filtered, "seq", split_axis=0, concat_axis=0, tiled=True)
     if number != 128:
         returned = jnp.transpose(returned, (1, 0, 2)).reshape(count, width // 128, 128)
         returned = jnp.transpose(returned, (1, 0, 2))
-    attn, asum = attention(heads_query, keys, values)
+    attn, asum = attention(heads_query, [heads_key] + keys, [heads_value] + values)
     msum = mixer_sums(mixer_query, returned)
     asum = lax.psum(asum, "head")
     msum = lax.psum(msum, "head")

time: 226 us -> 162 us (0.72)
  the two profiles are of different devices: /device:TPU:20 before, /device:TPU:16 now
where the time goes in v2:
time: 162 us; the launch traced here: 161 us
  waiting for transfers between devices  58.8 us (36%)
  Pallas kernels  58.7 us (36%)
  starting transfers between devices  31.1 us (19%)
  blocking collectives  9.4 us (6%)
  local copies, waits for them, and re-layouts  2.78 us (2%)
    ppermute x6, waiting for transfers between devices, routed(): lax.ppermute(block, 'seq', [(i, j) for i, j in pairs if 0 <= j < count])  41.4 us
    pallas_call x1, Pallas kernels, long_conv(): pl.pallas_call(functools.partial(conv_kernel_body, outer), in_specs=[VMEM...  21.8 us
    all_to_all x1, waiting for transfers between devices, on_device(): lax.all_to_all(filtered, 'seq', split_axis=0, concat_axis=0, tiled=True)  12.8 us
    all_to_all x1, starting transfers between devices, on_device(): lax.all_to_all(filtered, 'seq', split_axis=0, concat_axis=0, tiled=True)  12.8 us
    pallas_call x1, Pallas kernels, attention(): pl.pallas_call(attention_kernel, grid=(width // step,), in_specs=[block]...  12.3 us
    pallas_call x1, Pallas kernels, kernel_spectrum(): pl.pallas_call(functools.partial(kernel_spectrum_kernel, outer), in_specs...  11.5 us
    ppermute x6, starting transfers between devices, routed(): lax.ppermute(block, 'seq', [(i, j) for i, j in pairs if 0 <= j < count])  10.2 us
    psum x1, blocking collectives, on_device(): asum = lax.psum(asum, 'head')  9.4 us
  transfers between devices with their start and end apart: 9, of which 4 were waited for; matrix products, arithmetic and copies ran while one was open for 0% of the time, Pallas kernels for 32%

profile of v2, /device:TPU:16, one launch (start us, length us, event | category | flops | bytes accessed | tf_op | source)
XLA Modules:
  0.0 161.0 jit_solution(13189826955613771357)
XLA Ops:
  0.0 0.8 slice.3
  0.9 2.1 %collective-permute-start = (bf16[16,2048]{1,0:T(8,128)(2,1)S(1)}, bf16[16,2048]{1,0:T(8,128)(2,1)S(1)}, u32[]{:S(2)}, u32[]{:S(2)}) collective-permute-start(bf16[16,2048]{1,0:T(8,128)(2,1)S(1)} %slice.3), channel_id=1, source_target_pairs={{0,2},{2,4},{4,6},{6,8},{8,10},{10,12},{12,14},{14,16},{16,18},{18... | collective-permute-start | bytes 196616 | tf_op jit(solution)/shard_map/ppermute | solution.py:30
  2.9 4.6 %collective-permute-done.before_ref = bf16[16,2048]{1,0:T(8,128)(2,1)S(1)} collective-permute-done((bf16[16,2048]{1,0:T(8,128)(2,1)S(1)}, bf16[16,2048]{1,0:T(8,128)(2,1)S(1)}, u32[]{:S(2)}, u32[]{:S(2)}) %collective-permute-start) | collective-permute-done | bytes 65568 | tf_op jit(solution)/shard_map/ppermute | solution.py:30
  7.5 2.5 %collective-permute-start.1 = (bf16[256,2048]{1,0:T(8,128)(2,1)}, bf16[256,2048]{1,0:T(8,128)(2,1)}, u32[]{:S(2)}, u32[]{:S(2)}) collective-permute-start(bf16[256,2048]{1,0:T(8,128)(2,1)} %refs_1_), channel_id=1, source_target_pairs={{0,4},{2,6},{4,8},{6,10},{8,12},{10,14},{12,16},{14,18},{16,20},{1... | collective-permute-start | bytes 3145736 | tf_op jit(solution)/shard_map/ppermute | solution.py:35
  10.0 0.0 copy-done.2
  10.0 5.8 %shift.1 = bf16[16,256,128]{2,1,0:T(8,128)(2,1)} custom-call(bf16[256,2048]{1,0:T(8,128)(2,1)} %key_ref.1, bf16[16,2048]{1,0:T(8,128)(2,1)} %copy-done.2, bf16[256,2048]{1,0:T(8,128)(2,1)} %value_ref.1, f32[8,2048]{1,0:T(8,128)} %taps_ref.1), custom_call_target="tpu_custom_call" | custom-call | tf_op jit(solution)/shard_map/shift/pallas_call | solution.py:61
  15.8 6.1 %all-to-all-start = ((bf16[16,256,128]{2,1,0:T(8,128)(2,1)}), bf16[16,256,128]{2,1,0:T(8,128)(2,1)S(1)}, u32[]{:S(2)}, u32[]{:S(2)}) async-start(bf16[16,256,128]{2,1,0:T(8,128)(2,1)} %shift.1), calls=%async_computation | async-start | bytes 2097152 | tf_op jit(solution)/shard_map/all_to_all | solution.py:415
  21.9 0.0 copy-done.5
  21.9 3.4 %collective-permute-start.4 = (bf16[256,2048]{1,0:T(8,128)(2,1)S(1)}, bf16[256,2048]{1,0:T(8,128)(2,1)}, u32[]{:S(2)}, u32[]{:S(2)}) collective-permute-start(bf16[256,2048]{1,0:T(8,128)(2,1)S(1)} %copy-done.5), channel_id=1, source_target_pairs={{0,4},{2,6},{4,8},{6,10},{8,12},{10,14},{12,16},{14,18},{16,20},{1... | collective-permute-start | bytes 3145736 | tf_op jit(solution)/shard_map/ppermute | solution.py:35
  25.2 0.0 copy-done.4
  25.3 1.9 %collective-permute-start.3 = (bf16[256,2048]{1,0:T(8,128)(2,1)S(1)}, bf16[256,2048]{1,0:T(8,128)(2,1)}, u32[]{:S(2)}, u32[]{:S(2)}) collective-permute-start(bf16[256,2048]{1,0:T(8,128)(2,1)S(1)} %copy-done.4), channel_id=1, source_target_pairs={{0,2},{2,8},{4,6},{6,12},{8,10},{10,16},{12,14},{14,20},{16,18},{1... | collective-permute-start | bytes 3145736 | tf_op jit(solution)/shard_map/ppermute | solution.py:35
  27.2 14.3 %collective-permute-done.1.refs_8_.refs_2_ = bf16[256,2048]{1,0:T(8,128)(2,1)} collective-permute-done((bf16[256,2048]{1,0:T(8,128)(2,1)}, bf16[256,2048]{1,0:T(8,128)(2,1)}, u32[]{:S(2)}, u32[]{:S(2)}) %collective-permute-start.1) | collective-permute-done | bytes 1048608 | tf_op jit(solution)/shard_map/ppermute | solution.py:35
  41.5 0.0 collective-permute-start.2
  41.5 11.5 %kernel_spectrum.1.refs_1_ = f32[32,256,128]{2,1,0:T(8,128)} custom-call(f32[128,4096]{1,0:T(8,128)} %ker_ref.1, bf16[256,256]{1,0:T(8,128)(2,1)} %constant.12.clone.gh_ref.refs_2_, bf16[256,256]{1,0:T(8,128)(2,1)} %constant.13.clone.gl_ref.refs_3_, f32[128,32]{1,0:T(8,128)} %constant.14.clone.c_ref.refs_6_, f32[128,32]{1,0:T(8,128)} %constant.15.clone.s_ref.refs_7_), custom_call_target="tpu_custom_call" | custom-call | flops 6000000000 | bytes 7340032 | tf_op jit(solution)/shard_map/kernel_spectrum/pallas_call | solution.py:237
  53.0 2.4 %collective-permute-start.6 = (bf16[256,2048]{1,0:T(8,128)(2,1)S(1)}, bf16[256,2048]{1,0:T(8,128)(2,1)}, u32[]{:S(2)}, u32[]{:S(2)}) collective-permute-start(bf16[256,2048]{1,0:T(8,128)(2,1)S(1)} %copy-done.5), channel_id=1, source_target_pairs={{0,2},{2,8},{4,6},{6,12},{8,10},{10,16},{12,14},{14,20},{16,18},{1... | collective-permute-start | bytes 3145736 | tf_op jit(solution)/shard_map/ppermute | solution.py:35
  55.4 27.1 %collective-permute-done.4.refs_6_ = bf16[256,2048]{1,0:T(8,128)(2,1)} collective-permute-done((bf16[256,2048]{1,0:T(8,128)(2,1)S(1)}, bf16[256,2048]{1,0:T(8,128)(2,1)}, u32[]{:S(2)}, u32[]{:S(2)}) %collective-permute-start.4) | collective-permute-done | bytes 1048608 | tf_op jit(solution)/shard_map/ppermute | solution.py:35
  82.5 0.0 collective-permute-start.5
  82.5 0.0 collective-permute-done.3.refs_10_.refs_4_
  82.5 0.0 all-to-all-done
  82.5 0.0 copy-start.1
  82.5 0.0 collective-permute-done.2.refs_9_.refs_3_
  82.6 0.9 copy-done.1
  83.5 21.8 %long_conv.1 = bf16[4096,128]{1,0:T(8,128)(2,1)} custom-call(bf16[4096,128]{1,0:T(8,128)(2,1)} %bitcast.4, f32[32,256,128]{2,1,0:T(8,128)} %kernel_spectrum.1.refs_1_, bf16[256,256]{1,0:T(8,128)(2,1)} %constant.12.clone.gh_ref.refs_2_, bf16[256,256]{1,0:T(8,128)(2,1)} %constant.13.clone.gl_ref.refs_3_, bf16[256,256]{1,0:T(8,128)(2,1)} %constant.16.clone.refs_4_, ...), custom_call_target="tpu_custom_call" | custom-call | flops 12000000000 | bytes 7340032 | tf_op jit(solution)/shard_map/long_conv/pallas_call | solution.py:257
  105.3 0.0 collective-permute-done.6.refs_8_
  105.3 0.0 collective-permute-done.5.refs_7_
  105.3 12.8 %all-to-all-start.1 = ((bf16[16,256,128]{2,1,0:T(8,128)(2,1)}), bf16[16,256,128]{2,1,0:T(8,128)(2,1)S(1)}, u32[]{:S(2)}, u32[]{:S(2)}) async-start(bf16[16,256,128]{2,1,0:T(8,128)(2,1)} %bitcast.5), calls=%async_computation.1 | async-start | bytes 2097152 | tf_op jit(solution)/shard_map/all_to_all | solution.py:422
  118.1 12.3 %attention.1 = (f32[256,2048]{1,0:T(8,128)}, f32[8,256]{1,0:T(8,128)}) custom-call(bf16[256,2048]{1,0:T(8,128)(2,1)} %refs_0_.1, bf16[256,2048]{1,0:T(8,128)(2,1)} %refs_1_, bf16[256,2048]{1,0:T(8,128)(2,1)} %collective-permute-done.1.refs_8_.refs_2_, bf16[256,2048]{1,0:T(8,128)(2,1)} %collective-permute-done.2.refs_9_.refs_3_, ...), custom_call_target="tpu_custom_call" | custom-call | flops 5000000000 | bytes 11534336 | tf_op jit(solution)/shard_map/attention/pallas_call | solution.py:330
  130.4 12.8 %all-to-all-done.1.filtered_ref = bf16[16,256,128]{2,1,0:T(8,128)(2,1)S(1)} async-done(((bf16[16,256,128]{2,1,0:T(8,128)(2,1)}), bf16[16,256,128]{2,1,0:T(8,128)(2,1)S(1)}, u32[]{:S(2)}, u32[]{:S(2)}) %all-to-all-start.1) | async-done | bytes 1048608 | tf_op jit(solution)/shard_map/all_to_all | solution.py:422
  143.2 1.0 copy-done
  144.2 2.7 %mixer_sums.1 = f32[8,256]{1,0:T(8,128)} custom-call(bf16[256,2048]{1,0:T(8,128)(2,1)} %query_ref.3, bf16[16,256,128]{2,1,0:T(8,128)(2,1)} %copy-done), custom_call_target="tpu_custom_call" | custom-call | tf_op jit(solution)/shard_map/mixer_sums/pallas_call | solution.py:356
  146.9 9.4 %all-reduce = (f32[8,256]{1,0:T(8,128)}, f32[8,256]{1,0:T(8,128)}) all-reduce(f32[8,256]{1,0:T(8,128)S(1)} %copy-done.3, f32[8,256]{1,0:T(8,128)} %mixer_sums.1), channel_id=1, replica_groups=mesh['seq'=16,'head'=2] {'head'}, use_global_device_ids=true, to_apply=%region_0.0 | all-reduce | flops 4096 | bytes 32768 | tf_op jit(solution)/shard_map/psum | solution.py:428
  156.3 4.7 %join.1 = bf16[256,2048]{1,0:T(8,128)(2,1)} custom-call(f32[256,2048]{1,0:T(8,128)} %get-tuple-element.20.attn_ref, bf16[256,2048]{1,0:T(8,128)(2,1)} %query_ref.3, bf16[16,256,128]{2,1,0:T(8,128)(2,1)} %copy-done, f32[8,256]{1,0:T(8,128)} %get-tuple-element.23.asum_ref, f32[8,256]{1,0:T(8,128)} %get-tuple-element.24.msum_ref, f32[1,2048]{1,0:T(1,128)} %bitcast.6, ...), custom_call_target="tpu_custom_call" | custom-call | tf_op jit(solution)/shard_map/join/pallas_call | solution.py:383
  (6 shorter events, 0.0 us)
Async XLA Ops:
  0.8 21.0 %copy-start.5 = (bf16[256,2048]{1,0:T(8,128)(2,1)S(1)}, bf16[256,2048]{1,0:T(8,128)(2,1)}, u32[]{:S(2)}) copy-start(bf16[256,2048]{1,0:T(8,128)(2,1)} %refs_5_.1) | copy-start | bytes 3145732
  0.8 24.4 %copy-start.4 = (bf16[256,2048]{1,0:T(8,128)(2,1)S(1)}, bf16[256,2048]{1,0:T(8,128)(2,1)}, u32[]{:S(2)}) copy-start(bf16[256,2048]{1,0:T(8,128)(2,1)} %refs_1_) | copy-start | bytes 3145732
  0.9 6.6 %collective-permute-start = (bf16[16,2048]{1,0:T(8,128)(2,1)S(1)}, bf16[16,2048]{1,0:T(8,128)(2,1)S(1)}, u32[]{:S(2)}, u32[]{:S(2)}) collective-permute-start(bf16[16,2048]{1,0:T(8,128)(2,1)S(1)} %slice.3), channel_id=1, source_target_pairs={{0,2},{2,4},{4,6},{6,8},{8,10},{10,12},{12,14},{14,16},{16,18},{18... | collective-permute-start | bytes 196616 | tf_op jit(solution)/shard_map/ppermute | solution.py:30
  7.5 2.5 %copy-start.2 = (bf16[16,2048]{1,0:T(8,128)(2,1)}, bf16[16,2048]{1,0:T(8,128)(2,1)S(1)}, u32[]{:S(2)}) copy-start(bf16[16,2048]{1,0:T(8,128)(2,1)S(1)} %collective-permute-done.before_ref) | copy-start | bytes 196612
  7.5 34.0 %collective-permute-start.1 = (bf16[256,2048]{1,0:T(8,128)(2,1)}, bf16[256,2048]{1,0:T(8,128)(2,1)}, u32[]{:S(2)}, u32[]{:S(2)}) collective-permute-start(bf16[256,2048]{1,0:T(8,128)(2,1)} %refs_1_), channel_id=1, source_target_pairs={{0,4},{2,6},{4,8},{6,10},{8,12},{10,14},{12,16},{14,18},{16,20},{1... | collective-permute-start | bytes 3145736 | tf_op jit(solution)/shard_map/ppermute | solution.py:35
  15.8 66.7 %all-to-all-start = ((bf16[16,256,128]{2,1,0:T(8,128)(2,1)}), bf16[16,256,128]{2,1,0:T(8,128)(2,1)S(1)}, u32[]{:S(2)}, u32[]{:S(2)}) async-start(bf16[16,256,128]{2,1,0:T(8,128)(2,1)} %shift.1), calls=%async_computation | async-start | bytes 2097152 | tf_op jit(solution)/shard_map/all_to_all | solution.py:415
  21.9 60.7 %collective-permute-start.4 = (bf16[256,2048]{1,0:T(8,128)(2,1)S(1)}, bf16[256,2048]{1,0:T(8,128)(2,1)}, u32[]{:S(2)}, u32[]{:S(2)}) collective-permute-start(bf16[256,2048]{1,0:T(8,128)(2,1)S(1)} %copy-done.5), channel_id=1, source_target_pairs={{0,4},{2,6},{4,8},{6,10},{8,12},{10,14},{12,16},{14,18},{16,20},{1... | collective-permute-start | bytes 3145736 | tf_op jit(solution)/shard_map/ppermute | solution.py:35
  25.3 57.3 %collective-permute-start.3 = (bf16[256,2048]{1,0:T(8,128)(2,1)S(1)}, bf16[256,2048]{1,0:T(8,128)(2,1)}, u32[]{:S(2)}, u32[]{:S(2)}) collective-permute-start(bf16[256,2048]{1,0:T(8,128)(2,1)S(1)} %copy-done.4), channel_id=1, source_target_pairs={{0,2},{2,8},{4,6},{6,12},{8,10},{10,16},{12,14},{14,20},{16,18},{1... | collective-permute-start | bytes 3145736 | tf_op jit(solution)/shard_map/ppermute | solution.py:35
  41.5 41.1 %collective-permute-start.2 = (bf16[256,2048]{1,0:T(8,128)(2,1)}, bf16[256,2048]{1,0:T(8,128)(2,1)}, u32[]{:S(2)}, u32[]{:S(2)}) collective-permute-start(bf16[256,2048]{1,0:T(8,128)(2,1)} %collective-permute-done.1.refs_8_.refs_2_), channel_id=1, source_target_pairs={{0,2},{2,0},{4,6},{6,4},{8,10},{10,8},{12,14},{14,12},{16,18},{18,... | collective-permute-start | bytes 3145736 | tf_op jit(solution)/shard_map/ppermute | solution.py:35
  53.0 52.3 %collective-permute-start.6 = (bf16[256,2048]{1,0:T(8,128)(2,1)S(1)}, bf16[256,2048]{1,0:T(8,128)(2,1)}, u32[]{:S(2)}, u32[]{:S(2)}) collective-permute-start(bf16[256,2048]{1,0:T(8,128)(2,1)S(1)} %copy-done.5), channel_id=1, source_target_pairs={{0,2},{2,8},{4,6},{6,12},{8,10},{10,16},{12,14},{14,20},{16,18},{1... | collective-permute-start | bytes 3145736 | tf_op jit(solution)/shard_map/ppermute | solution.py:35
  82.5 22.7 %collective-permute-start.5 = (bf16[256,2048]{1,0:T(8,128)(2,1)}, bf16[256,2048]{1,0:T(8,128)(2,1)}, u32[]{:S(2)}, u32[]{:S(2)}) collective-permute-start(bf16[256,2048]{1,0:T(8,128)(2,1)} %collective-permute-done.4.refs_6_), channel_id=1, source_target_pairs={{0,2},{2,0},{4,6},{6,4},{8,10},{10,8},{12,14},{14,12},{16,18},{18,... | collective-permute-start | bytes 3145736 | tf_op jit(solution)/shard_map/ppermute | solution.py:35
  82.5 1.0 copy-start.1
  105.3 38.0 %all-to-all-start.1 = ((bf16[16,256,128]{2,1,0:T(8,128)(2,1)}), bf16[16,256,128]{2,1,0:T(8,128)(2,1)S(1)}, u32[]{:S(2)}, u32[]{:S(2)}) async-start(bf16[16,256,128]{2,1,0:T(8,128)(2,1)} %bitcast.5), calls=%async_computation.1 | async-start | bytes 2097152 | tf_op jit(solution)/shard_map/all_to_all | solution.py:422
  130.4 16.5 %copy-start.3 = (f32[8,256]{1,0:T(8,128)S(1)}, f32[8,256]{1,0:T(8,128)}, u32[]{:S(2)}) copy-start(f32[8,256]{1,0:T(8,128)} %get-tuple-element.22) | copy-start | bytes 24580
  143.2 1.0 copy-start

commit v3 on v2

--- a/solution.py
+++ b/solution.py
@@ -35,12 +35,22 @@
     return lax.ppermute(block, "seq", [(i, j) for i, j in pairs if 0 <= j < count])
 
 
-def earlier(block):
-    ids = range(lax.axis_size("seq"))
-    two = routed(block, [(i, i + 2) for i in ids])
-    cross = routed(block, [(i, i + 1 + 2 * (i % 2)) for i in ids])
-    swapped = routed(two, [(i, i + 1 - 2 * (i % 2)) for i in ids])
-    return [two, swapped, cross]
+def two_back(block):
+    return routed(block, [(i, i + 2) for i in range(lax.axis_size("seq"))])
+
+
+def cross_back(block):
+    return routed(block, [(i, i + 1 + 2 * (i % 2)) for i in range(lax.axis_size("seq"))])
+
+
+def swapped(block):
+    return routed(block, [(i, i + 1 - 2 * (i % 2)) for i in range(lax.axis_size("seq"))])
+
+
+def head_sum(part):
+    if lax.axis_size("head") != 2:
+        return lax.psum(part, "head")
+    return part + lax.ppermute(part, "head", [(0, 1), (1, 0)])
 
 
 def shift_kernel(key_ref, before_ref, value_ref, taps_ref, out_ref, ext_ref):
@@ -414,19 +424,25 @@
         ssm_input = jnp.transpose(ssm_input, (1, 0, 2))
     signal = lax.all_to_all(ssm_input, "seq", split_axis=0, concat_axis=0, tiled=True)
     spectrum = kernel_spectrum(conv_kernel)
-    keys = earlier(heads_key)
-    values = earlier(heads_value)
-    filtered = long_conv(signal.reshape(length, number), spectrum, keys)
-    filtered, *values = lax.optimization_barrier((filtered, *values))
+    key_two = two_back(heads_key)
+    value_two = two_back(heads_value)
+    key_cross = cross_back(heads_key)
+    value_cross = cross_back(heads_value)
+    filtered = long_conv(signal.reshape(length, number), spectrum, [key_two])
+    filtered, key_two, key_cross, value_two, value_cross = lax.optimization_barrier(
+        (filtered, key_two, key_cross, value_two, value_cross)
+    )
+    keys = [heads_key, key_two, swapped(key_two), key_cross]
+    values = [heads_value, value_two, swapped(value_two), value_cross]
     filtered = filtered.reshape(devices, count, number)
     returned = lax.all_to_all(filtered, "seq", split_axis=0, concat_axis=0, tiled=True)
     if number != 128:
         returned = jnp.transpose(returned, (1, 0, 2)).reshape(count, width // 128, 128)
         returned = jnp.transpose(returned, (1, 0, 2))
-    attn, asum = attention(heads_query, [heads_key] + keys, [heads_value] + values)
+    attn, asum = attention(heads_query, keys, values)
     msum = mixer_sums(mixer_query, returned)
-    asum = lax.psum(asum, "head")
-    msum = lax.psum(msum, "head")
+    asum = head_sum(asum)
+    msum = head_sum(msum)
     return join(attn, mixer_query, returned, asum, msum, beta_attention, beta_mixer)
 
 

time: 162 us -> 156 us (0.963)
  waiting for transfers between devices: 58.8 us -> 42.1 us
  starting transfers between devices: 31.1 us -> 47.6 us
  blocking collectives: 9.4 us -> 0 us
  other arithmetic: 0 us -> 1.9 us
  local copies, waits for them, and re-layouts: 2.78 us -> 4.41 us
    all_to_all x1, starting transfers between devices: 12.8 us -> 25.9 us  [on_device(): lax.all_to_all(filtered, 'seq', split_axis=0, concat_axis=0, tiled=True)]
    ppermute x6, waiting for transfers between devices: 41.4 us -> 29.8 us  [routed(): lax.ppermute(block, 'seq', [(i, j) for i, j in pairs if 0 <= j < count])]
    psum x1 -> x0, blocking collectives: 9.4 us -> none  [on_device(): asum = lax.psum(asum, 'head')]
    all_to_all x1, waiting for transfers between devices: 12.8 us -> 5.94 us  [on_device(): lax.all_to_all(filtered, 'seq', split_axis=0, concat_axis=0, tiled=True)]
    ppermute x0 -> x2, starting transfers between devices: none -> 3.05 us  [head_sum(): return part + lax.ppermute(part, 'head', [(0, 1), (1, 0)])]
    add x0 -> x2, other arithmetic: none -> 1.9 us  [head_sum(): return part + lax.ppermute(part, 'head', [(0, 1), (1, 0)])]
    ppermute x0 -> x2, waiting for transfers between devices: none -> 1.77 us  [head_sum(): return part + lax.ppermute(part, 'head', [(0, 1), (1, 0)])]
    unnamed x12 -> x16, local copies, waits for them, and re-layouts: 1.94 us -> 3.56 us
  transfers between devices with their start and end apart: 9 -> 11, of which waited for: 4 -> 6; matrix products, arithmetic and copies ran while one was open for 0% -> 0% of each run, Pallas kernels for 32% -> 31%
where the time goes in v3:
time: 156 us; the launch traced here: 155 us
  Pallas kernels  58.7 us (38%)
  starting transfers between devices  47.6 us (31%)
  waiting for transfers between devices  42.1 us (27%)
  local copies, waits for them, and re-layouts  4.41 us (3%)
  other arithmetic  1.9 us (1%)
    ppermute x6, waiting for transfers between devices, routed(): lax.ppermute(block, 'seq', [(i, j) for i, j in pairs if 0 <= j < count])  29.8 us
    all_to_all x1, starting transfers between devices, on_device(): lax.all_to_all(filtered, 'seq', split_axis=0, concat_axis=0, tiled=True)  25.9 us
    pallas_call x1, Pallas kernels, long_conv(): pl.pallas_call(functools.partial(conv_kernel_body, outer), in_specs=[VMEM...  21.8 us
    pallas_call x1, Pallas kernels, attention(): pl.pallas_call(attention_kernel, grid=(width // step,), in_specs=[block]...  12.3 us
    pallas_call x1, Pallas kernels, kernel_spectrum(): pl.pallas_call(functools.partial(kernel_spectrum_kernel, outer), in_specs...  11.5 us
    ppermute x6, starting transfers between devices, routed(): lax.ppermute(block, 'seq', [(i, j) for i, j in pairs if 0 <= j < count])  11.3 us
    all_to_all x1, waiting for transfers between devices, on_device(): lax.all_to_all(filtered, 'seq', split_axis=0, concat_axis=0, tiled=True)  5.94 us
    pallas_call x1, Pallas kernels, shift_filter(): pl.pallas_call(shift_kernel, grid=(width // step,), in_specs=[pl.BlockSpe...  5.76 us
  transfers between devices with their start and end apart: 11, of which 6 were waited for; matrix products, arithmetic and copies ran while one was open for 0% of the time, Pallas kernels for 31%

profile of v3, /device:TPU:16, one launch (start us, length us, event | category | flops | bytes accessed | tf_op | source)
XLA Modules:
  0.0 154.8 jit_solution(13972723323839903173)
XLA Ops:
  0.0 0.8 slice.3
  0.8 2.0 %collective-permute-start = (bf16[16,2048]{1,0:T(8,128)(2,1)S(1)}, bf16[16,2048]{1,0:T(8,128)(2,1)S(1)}, u32[]{:S(2)}, u32[]{:S(2)}) collective-permute-start(bf16[16,2048]{1,0:T(8,128)(2,1)S(1)} %slice.3), channel_id=1, source_target_pairs={{0,2},{2,4},{4,6},{6,8},{8,10},{10,12},{12,14},{14,16},{16,18},{18... | collective-permute-start | bytes 196616 | tf_op jit(solution)/shard_map/ppermute | solution.py:30
  2.9 4.6 %collective-permute-done.before_ref = bf16[16,2048]{1,0:T(8,128)(2,1)S(1)} collective-permute-done((bf16[16,2048]{1,0:T(8,128)(2,1)S(1)}, bf16[16,2048]{1,0:T(8,128)(2,1)S(1)}, u32[]{:S(2)}, u32[]{:S(2)}) %collective-permute-start) | collective-permute-done | bytes 65568 | tf_op jit(solution)/shard_map/ppermute | solution.py:30
  7.5 0.6 copy-done.2
  8.1 5.8 %shift.1 = bf16[16,256,128]{2,1,0:T(8,128)(2,1)} custom-call(bf16[256,2048]{1,0:T(8,128)(2,1)} %key_ref.1, bf16[16,2048]{1,0:T(8,128)(2,1)} %copy-done.2, bf16[256,2048]{1,0:T(8,128)(2,1)} %value_ref.1, f32[8,2048]{1,0:T(8,128)} %taps_ref.1), custom_call_target="tpu_custom_call" | custom-call | tf_op jit(solution)/shard_map/shift/pallas_call | solution.py:71
  13.8 5.3 %all-to-all-start = ((bf16[16,256,128]{2,1,0:T(8,128)(2,1)}), bf16[16,256,128]{2,1,0:T(8,128)(2,1)S(1)}, u32[]{:S(2)}, u32[]{:S(2)}) async-start(bf16[16,256,128]{2,1,0:T(8,128)(2,1)} %shift.1), calls=%async_computation | async-start | bytes 2097152 | tf_op jit(solution)/shard_map/all_to_all | solution.py:425
  19.1 0.0 copy-start.5
  19.1 3.5 %collective-permute-start.1 = (bf16[256,2048]{1,0:T(8,128)(2,1)S(1)}, bf16[256,2048]{1,0:T(8,128)(2,1)}, u32[]{:S(2)}, u32[]{:S(2)}) collective-permute-start(bf16[256,2048]{1,0:T(8,128)(2,1)S(1)} %copy-done.4), channel_id=1, source_target_pairs={{0,4},{2,6},{4,8},{6,10},{8,12},{10,14},{12,16},{14,18},{16,20},{1... | collective-permute-start | bytes 3145736 | tf_op jit(solution)/shard_map/ppermute | solution.py:35
  22.7 11.5 %kernel_spectrum.1.refs_1_ = f32[32,256,128]{2,1,0:T(8,128)} custom-call(f32[128,4096]{1,0:T(8,128)} %ker_ref.1, bf16[256,256]{1,0:T(8,128)(2,1)} %constant.12.clone.gh_ref.refs_2_, bf16[256,256]{1,0:T(8,128)(2,1)} %constant.13.clone.gl_ref.refs_3_, f32[128,32]{1,0:T(8,128)} %constant.14.clone.c_ref.refs_6_, f32[128,32]{1,0:T(8,128)} %constant.15.clone.s_ref.refs_7_), custom_call_target="tpu_custom_call" | custom-call | flops 6000000000 | bytes 7340032 | tf_op jit(solution)/shard_map/kernel_spectrum/pallas_call | solution.py:247
  34.2 1.9 %collective-permute-start.2 = (bf16[256,2048]{1,0:T(8,128)(2,1)S(1)}, bf16[256,2048]{1,0:T(8,128)(2,1)}, u32[]{:S(2)}, u32[]{:S(2)}) collective-permute-start(bf16[256,2048]{1,0:T(8,128)(2,1)S(1)} %copy-done.4), channel_id=1, source_target_pairs={{0,2},{2,8},{4,6},{6,12},{8,10},{10,16},{12,14},{14,20},{16,18},{1... | collective-permute-start | bytes 3145736 | tf_op jit(solution)/shard_map/ppermute | solution.py:35
  36.1 3.4 %collective-permute-start.3 = (bf16[256,2048]{1,0:T(8,128)(2,1)S(1)}, bf16[256,2048]{1,0:T(8,128)(2,1)}, u32[]{:S(2)}, u32[]{:S(2)}) collective-permute-start(bf16[256,2048]{1,0:T(8,128)(2,1)S(1)} %copy-done.5), channel_id=1, source_target_pairs={{0,4},{2,6},{4,8},{6,10},{8,12},{10,14},{12,16},{14,18},{16,20},{1... | collective-permute-start | bytes 3145736 | tf_op jit(solution)/shard_map/ppermute | solution.py:35
  39.5 2.0 %collective-permute-start.4 = (bf16[256,2048]{1,0:T(8,128)(2,1)S(1)}, bf16[256,2048]{1,0:T(8,128)(2,1)}, u32[]{:S(2)}, u32[]{:S(2)}) collective-permute-start(bf16[256,2048]{1,0:T(8,128)(2,1)S(1)} %copy-done.5), channel_id=1, source_target_pairs={{0,2},{2,8},{4,6},{6,12},{8,10},{10,16},{12,14},{14,20},{16,18},{1... | collective-permute-start | bytes 3145736 | tf_op jit(solution)/shard_map/ppermute | solution.py:35
  41.5 25.9 %collective-permute-done.1.refs_8_.refs_2_ = bf16[256,2048]{1,0:T(8,128)(2,1)} collective-permute-done((bf16[256,2048]{1,0:T(8,128)(2,1)S(1)}, bf16[256,2048]{1,0:T(8,128)(2,1)}, u32[]{:S(2)}, u32[]{:S(2)}) %collective-permute-start.1) | collective-permute-done | bytes 1048608 | tf_op jit(solution)/shard_map/ppermute | solution.py:35
  67.4 0.0 all-to-all-done
  67.4 1.0 copy-done.1
  68.4 21.8 %long_conv.1 = bf16[4096,128]{1,0:T(8,128)(2,1)} custom-call(bf16[4096,128]{1,0:T(8,128)(2,1)} %bitcast.5, f32[32,256,128]{2,1,0:T(8,128)} %kernel_spectrum.1.refs_1_, bf16[256,256]{1,0:T(8,128)(2,1)} %constant.12.clone.gh_ref.refs_2_, bf16[256,256]{1,0:T(8,128)(2,1)} %constant.13.clone.gl_ref.refs_3_, bf16[256,256]{1,0:T(8,128)(2,1)} %constant.16.clone.refs_4_, ...), custom_call_target="tpu_custom_call" | custom-call | flops 12000000000 | bytes 7340032 | tf_op jit(solution)/shard_map/long_conv/pallas_call | solution.py:267
  90.2 25.9 %all-to-all-start.1 = ((bf16[16,256,128]{2,1,0:T(8,128)(2,1)}), bf16[16,256,128]{2,1,0:T(8,128)(2,1)S(1)}, u32[]{:S(2)}, u32[]{:S(2)}) async-start(bf16[16,256,128]{2,1,0:T(8,128)(2,1)} %bitcast.4), calls=%async_computation.1 | async-start | bytes 2097152 | tf_op jit(solution)/shard_map/all_to_all | solution.py:438
  116.1 0.1 collective-permute-start.5
  116.3 0.4 collective-permute-start.6
  116.6 2.4 %collective-permute-done.5.refs_3_ = bf16[256,2048]{1,0:T(8,128)(2,1)S(1)} collective-permute-done((bf16[256,2048]{1,0:T(8,128)(2,1)}, bf16[256,2048]{1,0:T(8,128)(2,1)S(1)}, u32[]{:S(2)}, u32[]{:S(2)}) %collective-permute-start.5) | collective-permute-done | bytes 1048608 | tf_op jit(solution)/shard_map/ppermute | solution.py:35
  119.0 1.5 collective-permute-done.6.refs_7_
  120.5 1.0 copy-done.7
  121.5 12.3 %attention.1 = (f32[256,2048]{1,0:T(8,128)}, f32[8,256]{1,0:T(8,128)}) custom-call(bf16[256,2048]{1,0:T(8,128)(2,1)} %refs_0_.1, bf16[256,2048]{1,0:T(8,128)(2,1)} %refs_1_, bf16[256,2048]{1,0:T(8,128)(2,1)} %collective-permute-done.1.refs_8_.refs_2_, bf16[256,2048]{1,0:T(8,128)(2,1)} %copy-done.6, bf16[256,2048]{1,0:T(8,128)(2,1)} %collective-permute-done.2.refs_4_, ...), custom_call_target="tpu_custom_call" | custom-call | flops 5000000000 | bytes 11534336 | tf_op jit(solution)/shard_map/attention/pallas_call | solution.py:340
  133.8 1.6 %collective-permute-start.7 = (f32[8,256]{1,0:T(8,128)}, f32[8,256]{1,0:T(8,128)S(1)}, u32[]{:S(2)}, u32[]{:S(2)}) collective-permute-start(f32[8,256]{1,0:T(8,128)} %get-tuple-element.24), channel_id=1, source_target_pairs={{0,1},{1,0},{2,3},{3,2},{4,5},{5,4},{6,7},{7,6},{8,9},{9,8},{10,11... | collective-permute-start | bytes 24584 | tf_op jit(solution)/shard_map/ppermute | solution.py:53
  135.4 5.9 %all-to-all-done.1.filtered_ref = bf16[16,256,128]{2,1,0:T(8,128)(2,1)S(1)} async-done(((bf16[16,256,128]{2,1,0:T(8,128)(2,1)}), bf16[16,256,128]{2,1,0:T(8,128)(2,1)S(1)}, u32[]{:S(2)}, u32[]{:S(2)}) %all-to-all-start.1) | async-done | bytes 1048608 | tf_op jit(solution)/shard_map/all_to_all | solution.py:438
  141.3 1.0 copy-done
  142.3 2.7 %mixer_sums.1 = f32[8,256]{1,0:T(8,128)} custom-call(bf16[256,2048]{1,0:T(8,128)(2,1)} %query_ref.3, bf16[16,256,128]{2,1,0:T(8,128)(2,1)} %copy-done), custom_call_target="tpu_custom_call" | custom-call | tf_op jit(solution)/shard_map/mixer_sums/pallas_call | solution.py:366
  144.9 1.5 collective-permute-start.8
  146.4 0.6 add.6.asum_ref
  147.0 1.8 %collective-permute-done.8 = f32[8,256]{1,0:T(8,128)S(1)} collective-permute-done((f32[8,256]{1,0:T(8,128)}, f32[8,256]{1,0:T(8,128)S(1)}, u32[]{:S(2)}, u32[]{:S(2)}) %collective-permute-start.8) | collective-permute-done | bytes 8224 | tf_op jit(solution)/shard_map/ppermute | solution.py:53
  148.8 1.3 add.7.msum_ref
  150.1 4.7 %join.1 = bf16[256,2048]{1,0:T(8,128)(2,1)} custom-call(f32[256,2048]{1,0:T(8,128)} %get-tuple-element.22.attn_ref, bf16[256,2048]{1,0:T(8,128)(2,1)} %query_ref.3, bf16[16,256,128]{2,1,0:T(8,128)(2,1)} %copy-done, f32[8,256]{1,0:T(8,128)} %add.6.asum_ref, f32[8,256]{1,0:T(8,128)} %add.7.msum_ref, f32[1,2048]{1,0:T(1,128)} %bitcast.6, f32[1,2048]{1,0:T(1,128)} %bitcast.7), custom_call_target="tpu_custom_call" | custom-call | tf_op jit(solution)/shard_map/join/pallas_call | solution.py:393
  (15 shorter events, 0.0 us)
Async XLA Ops:
  0.8 18.3 %copy-start.4 = (bf16[256,2048]{1,0:T(8,128)(2,1)S(1)}, bf16[256,2048]{1,0:T(8,128)(2,1)}, u32[]{:S(2)}) copy-start(bf16[256,2048]{1,0:T(8,128)(2,1)} %refs_1_) | copy-start | bytes 3145732
  0.8 6.6 %collective-permute-start = (bf16[16,2048]{1,0:T(8,128)(2,1)S(1)}, bf16[16,2048]{1,0:T(8,128)(2,1)S(1)}, u32[]{:S(2)}, u32[]{:S(2)}) collective-permute-start(bf16[16,2048]{1,0:T(8,128)(2,1)S(1)} %slice.3), channel_id=1, source_target_pairs={{0,2},{2,4},{4,6},{6,8},{8,10},{10,12},{12,14},{14,16},{16,18},{18... | collective-permute-start | bytes 196616 | tf_op jit(solution)/shard_map/ppermute | solution.py:30
  7.5 0.6 copy-start.2
  13.8 53.6 %all-to-all-start = ((bf16[16,256,128]{2,1,0:T(8,128)(2,1)}), bf16[16,256,128]{2,1,0:T(8,128)(2,1)S(1)}, u32[]{:S(2)}, u32[]{:S(2)}) async-start(bf16[16,256,128]{2,1,0:T(8,128)(2,1)} %shift.1), calls=%async_computation | async-start | bytes 2097152 | tf_op jit(solution)/shard_map/all_to_all | solution.py:425
  19.1 16.9 %copy-start.5 = (bf16[256,2048]{1,0:T(8,128)(2,1)S(1)}, bf16[256,2048]{1,0:T(8,128)(2,1)}, u32[]{:S(2)}) copy-start(bf16[256,2048]{1,0:T(8,128)(2,1)} %refs_5_.1) | copy-start | bytes 3145732
  19.1 48.3 %collective-permute-start.1 = (bf16[256,2048]{1,0:T(8,128)(2,1)S(1)}, bf16[256,2048]{1,0:T(8,128)(2,1)}, u32[]{:S(2)}, u32[]{:S(2)}) collective-permute-start(bf16[256,2048]{1,0:T(8,128)(2,1)S(1)} %copy-done.4), channel_id=1, source_target_pairs={{0,4},{2,6},{4,8},{6,10},{8,12},{10,14},{12,16},{14,18},{16,20},{1... | collective-permute-start | bytes 3145736 | tf_op jit(solution)/shard_map/ppermute | solution.py:35
  34.2 56.0 %collective-permute-start.2 = (bf16[256,2048]{1,0:T(8,128)(2,1)S(1)}, bf16[256,2048]{1,0:T(8,128)(2,1)}, u32[]{:S(2)}, u32[]{:S(2)}) collective-permute-start(bf16[256,2048]{1,0:T(8,128)(2,1)S(1)} %copy-done.4), channel_id=1, source_target_pairs={{0,2},{2,8},{4,6},{6,12},{8,10},{10,16},{12,14},{14,20},{16,18},{1... | collective-permute-start | bytes 3145736 | tf_op jit(solution)/shard_map/ppermute | solution.py:35
  36.1 54.1 %collective-permute-start.3 = (bf16[256,2048]{1,0:T(8,128)(2,1)S(1)}, bf16[256,2048]{1,0:T(8,128)(2,1)}, u32[]{:S(2)}, u32[]{:S(2)}) collective-permute-start(bf16[256,2048]{1,0:T(8,128)(2,1)S(1)} %copy-done.5), channel_id=1, source_target_pairs={{0,4},{2,6},{4,8},{6,10},{8,12},{10,14},{12,16},{14,18},{16,20},{1... | collective-permute-start | bytes 3145736 | tf_op jit(solution)/shard_map/ppermute | solution.py:35
  39.5 50.7 %collective-permute-start.4 = (bf16[256,2048]{1,0:T(8,128)(2,1)S(1)}, bf16[256,2048]{1,0:T(8,128)(2,1)}, u32[]{:S(2)}, u32[]{:S(2)}) collective-permute-start(bf16[256,2048]{1,0:T(8,128)(2,1)S(1)} %copy-done.5), channel_id=1, source_target_pairs={{0,2},{2,8},{4,6},{6,12},{8,10},{10,16},{12,14},{14,20},{16,18},{1... | collective-permute-start | bytes 3145736 | tf_op jit(solution)/shard_map/ppermute | solution.py:35
  67.4 1.0 copy-start.1
  90.2 51.1 %all-to-all-start.1 = ((bf16[16,256,128]{2,1,0:T(8,128)(2,1)}), bf16[16,256,128]{2,1,0:T(8,128)(2,1)S(1)}, u32[]{:S(2)}, u32[]{:S(2)}) async-start(bf16[16,256,128]{2,1,0:T(8,128)(2,1)} %bitcast.4), calls=%async_computation.1 | async-start | bytes 2097152 | tf_op jit(solution)/shard_map/all_to_all | solution.py:438
  116.1 2.9 %collective-permute-start.5 = (bf16[256,2048]{1,0:T(8,128)(2,1)}, bf16[256,2048]{1,0:T(8,128)(2,1)S(1)}, u32[]{:S(2)}, u32[]{:S(2)}) collective-permute-start(bf16[256,2048]{1,0:T(8,128)(2,1)} %collective-permute-done.1.refs_8_.refs_2_), channel_id=1, source_target_pairs={{0,2},{2,0},{4,6},{6,4},{8,10},{10,8},{12,14},{14,12},{16,18},{18,... | collective-permute-start | bytes 3145736 | tf_op jit(solution)/shard_map/ppermute | solution.py:35
  116.3 4.2 %collective-permute-start.6 = (bf16[256,2048]{1,0:T(8,128)(2,1)}, bf16[256,2048]{1,0:T(8,128)(2,1)S(1)}, u32[]{:S(2)}, u32[]{:S(2)}) collective-permute-start(bf16[256,2048]{1,0:T(8,128)(2,1)} %collective-permute-done.3.refs_6_), channel_id=1, source_target_pairs={{0,2},{2,0},{4,6},{6,4},{8,10},{10,8},{12,14},{14,12},{16,18},{18,... | collective-permute-start | bytes 3145736 | tf_op jit(solution)/shard_map/ppermute | solution.py:35
  119.0 1.5 copy-start.6
  120.5 1.0 copy-start.7
  133.8 12.6 %copy-start.3 = (f32[8,256]{1,0:T(8,128)S(1)}, f32[8,256]{1,0:T(8,128)}, u32[]{:S(2)}) copy-start(f32[8,256]{1,0:T(8,128)} %get-tuple-element.24) | copy-start | bytes 24580
  133.8 12.6 %collective-permute-start.7 = (f32[8,256]{1,0:T(8,128)}, f32[8,256]{1,0:T(8,128)S(1)}, u32[]{:S(2)}, u32[]{:S(2)}) collective-permute-start(f32[8,256]{1,0:T(8,128)} %get-tuple-element.24), channel_id=1, source_target_pairs={{0,1},{1,0},{2,3},{3,2},{4,5},{5,4},{6,7},{7,6},{8,9},{9,8},{10,11... | collective-permute-start | bytes 24584 | tf_op jit(solution)/shard_map/ppermute | solution.py:53
  141.3 1.0 copy-start
  144.9 3.9 %collective-permute-start.8 = (f32[8,256]{1,0:T(8,128)}, f32[8,256]{1,0:T(8,128)S(1)}, u32[]{:S(2)}, u32[]{:S(2)}) collective-permute-start(f32[8,256]{1,0:T(8,128)} %mixer_sums.1), channel_id=1, source_target_pairs={{0,1},{1,0},{2,3},{3,2},{4,5},{5,4},{6,7},{7,6},{8,9},{9,8},{10,11... | collective-permute-start | bytes 24584 | tf_op jit(solution)/shard_map/ppermute | solution.py:53
